TPU v7x, 32 devices: a whole 2x2x4 slice. The times are simulated.
32 devices in a mesh: grp: 2 (over y), blk: 8 (over z, x), sub: 2 (over core).
Axes of the slice: x: 2, y: 2, z: 4, core: 2. Of those that a mesh axis runs over, the one named last changes fastest.
Arguments:
- log_rate: float32 [16384], P(('grp', 'blk')), parts along dimension 0, may hold values from -1 to 0.5
- log_state: float32 [16384], P(('grp', 'blk')), parts along dimension 0, may hold values from -1 to 1
- load: float32 [16384], P(('grp', 'blk')), parts along dimension 0, may hold values from 1 to 4
- a_sigma: float32 [16384], P(('grp', 'blk')), parts along dimension 0, may hold values from 0.5 to 2
- b_sigma: float32 [16384], P(('grp', 'blk')), parts along dimension 0, may hold values from 0.5 to 2
- log_dc: float32 [16384], P(('grp', 'blk')), parts along dimension 0, may hold values from -0.5 to 0.5
- near_field: float32 [64, 128, 128], P(('blk', 'sub')), may hold values from -0.25 to 2.5, as said below
- col_cluster: int32 [8, 2, 88], P(None, 'sub'), may hold values from 0 to 63, as said below
- row_cluster: int32 [8, 2, 88], P(None, 'sub'), may hold values from 0 to 63, as said below
- ranks: int32 [8, 2, 88], P('blk', 'sub'), may hold values from 6 to 48
- col_factor: float32 [8, 2, 88, 48, 128], P('blk', 'sub'), may hold values from -0.5 to 0.5
- row_factor: float32 [8, 2, 88, 48, 128], P('blk', 'sub'), may hold values from -0.24 to 0.24
Outputs:
- new_log_rate: float32 [16384], P(('grp', 'blk')), parts along dimension 0
- new_log_state: float32 [16384], P(('grp', 'blk')), parts along dimension 0
There are 2 independent parts, one for each index of `grp`. A program takes and returns all parts, laid end to end along the dimension named above; an argument that names none is the same for every part. Nothing has to cross between parts.
Inputs may be any that keep to these rules, and one draw needn't show every extreme that they name: `col_cluster`: cluster c holds elements c * 128 to c * 128 + 127 and lies on blk device c // 8. For every owner o and group s, at most 22 of the 88 blocks take their columns from clusters of one device, and exactly 22 from some device. `row_cluster`: for every owner o and group s, at most 22 of the 88 blocks write to row clusters of one device, and exactly 22 to some device. `near_field`: each diagonal entry is 1 or more, and the other entries of a row are small beside it.
All inputs are finite; a program needn't handle non-finite values.
Results may differ from a plain program's by a relative error of at most 0.0003.
Values sent between devices are 32-bit elements; how exact they have to be, the bound alone decides.
No kernel may reach another device: no remote copies, remote signals or barrier semaphores. Data moves between devices by JAX's collectives and lax.ppermute only.
A program may use at most 64 MiB of HBM per device.

v0:
```python
import jax
import jax.numpy as jnp
from jax import lax
from jax.sharding import PartitionSpec as P

precise = lax.Precision.HIGHEST
damping = 0.5
time_step = 0.25


def fault_rates(log_values, log_states, traction, load, a_sigma, b_sigma, log_dc):
    state_rate = jnp.exp(-log_states) - jnp.exp(log_values - log_dc)
    rate_rate = (load - traction - b_sigma * state_rate) / (a_sigma + damping * jnp.exp(log_values))
    return (rate_rate, state_rate)


def shards(
    log_rate,
    log_state,
    load,
    a_sigma,
    b_sigma,
    log_dc,
    near_field,
    col_cluster,
    row_cluster,
    ranks,
    col_factor,
    row_factor,
):
    owners = lax.axis_size("blk")
    device = lax.axis_index("blk")
    leaf = near_field.shape[1]
    per_device = log_rate.shape[0] // leaf
    near_count = near_field.shape[0]
    columns_all = col_cluster[:, 0, :]
    rows_all = row_cluster[:, 0, :]
    own_columns = lax.dynamic_index_in_dim(columns_all, device, 0, keepdims=False)
    own_rows = lax.dynamic_index_in_dim(rows_all, device, 0, keepdims=False)
    levels = jnp.arange(col_factor.shape[3], dtype=jnp.int32)
    rank_mask = levels[None, :] < ranks[0, 0][:, None]
    column_factor = col_factor[0, 0]
    row_local = row_factor[0, 0]
    near_start = lax.axis_index("sub") * near_count

    def traction_of(log_values):
        slip_rate = jnp.exp(log_values).reshape(per_device, leaf)
        near_input = lax.dynamic_slice_in_dim(slip_rate, near_start, near_count, 0)
        near_local = jnp.einsum("cij,cj->ci", near_field, near_input, precision=precise)
        near_part = lax.dynamic_update_slice_in_dim(
            jnp.zeros((per_device, leaf), jnp.float32), near_local, near_start, 0
        )
        gathered = lax.all_gather(slip_rate, "blk", axis=0, tiled=True)
        block_input = gathered[own_columns]
        coefficient = jnp.einsum("bkl,bl->bk", column_factor, block_input, precision=precise)
        coefficient = jnp.where(rank_mask, coefficient, 0.0)
        block_output = jnp.einsum("bkl,bk->bl", row_local, coefficient, precision=precise)
        far_term = (
            jnp.zeros((owners * per_device, leaf), jnp.float32).at[own_rows].add(block_output)
        )
        far_part = lax.psum_scatter(far_term, "blk", scatter_dimension=0, tiled=True)
        summed = lax.psum(near_part + far_part, "sub")
        return summed.reshape(-1)

    rate_one, state_one = fault_rates(
        log_rate, log_state, traction_of(log_rate), load, a_sigma, b_sigma, log_dc
    )
    mid_rate = log_rate + time_step * rate_one
    mid_state = log_state + time_step * state_one
    rate_two, state_two = fault_rates(
        mid_rate, mid_state, traction_of(mid_rate), load, a_sigma, b_sigma, log_dc
    )
    new_log_rate = log_rate + 0.5 * time_step * (rate_one + rate_two)
    new_log_state = log_state + 0.5 * time_step * (state_one + state_two)
    return (new_log_rate, new_log_state)


def solution(mesh):
    placed = (
        P(("grp", "blk")),
        P(("grp", "blk")),
        P(("grp", "blk")),
        P(("grp", "blk")),
        P(("grp", "blk")),
        P(("grp", "blk")),
        P(("blk", "sub"), None, None),
        P(None, "sub", None),
        P(None, "sub", None),
        P("blk", "sub", None),
        P("blk", "sub", None, None, None),
        P("blk", "sub", None, None, None),
    )
    return jax.shard_map(
        shards,
        mesh=mesh,
        in_specs=placed,
        out_specs=(P(("grp", "blk")), P(("grp", "blk"))),
        check_vma=False,
    )
```

profile of v0, /device:TPU:0, one launch (start us, length us, event | category | flops | bytes accessed | tf_op | source)
XLA Modules:
  0.0 163.0 jit_solution(2297558379166781981)
XLA Ops:
  0.6 0.0 copy-start
  0.6 0.0 copy-start.8
  0.7 1.4 dynamic-slice.4
  2.7 0.7 fusion.18
  3.4 0.7 fusion.19
  4.0 0.7 exponential_bitcast_fusion
  4.7 1.5 fusion.20
  6.2 32.2 %all_gather.6 = f32[64,128]{1,0:T(8,128)S(1)} all-gather(f32[8,128]{1,0:T(8,128)S(1)} %exponential_bitcast_fusion), channel_id=1, replica_groups=mesh['grp'=2,'blk'=8,'sub'=2] {'blk'}, dimensions={0}, use_global_device_ids=true | all-gather | bytes 36864 | tf_op jit(solution)/shard_map/all_gather | solution.py:53
  38.4 0.6 gather_fusion
  39.0 0.0 copy-start.2
  39.0 0.0 copy-start.3
  39.0 0.0 copy-start.4
  39.1 0.0 copy-start.5
  39.1 0.0 copy-start.6
  39.1 0.0 copy-start.7
  39.1 0.0 copy-start.1
  39.1 5.1 %fusion.6 = f32[88,1,48]{2,1,0:T(1,128)S(1)} fusion(f32[88,128,1]{1,2,0:T(1,128)S(1)} %bitcast.73, f32[1,1,88,48,128]{4,3,2,1,0:T(8,128)} %param.22), kind=kOutput, calls=%fused_computation.10 | convolution fusion | flops 6488064 | bytes 2224640 | tf_op jit(solution)/shard_map/bkl,bl->bk/dot_general | solution.py:55
  44.2 0.0 copy-done.8
  44.2 0.1 fusion.9
  44.3 0.0 copy-done
  44.3 1.9 %fusion.2 = f32[88,1,128]{2,1,0:T(1,128)S(1)} fusion(f32[88,48,1]{1,2,0:T(1,128)S(1)} %bitcast.75, f32[1,1,88,48,128]{4,3,2,1,0:T(8,128)S(1)} %copy-done), kind=kOutput, calls=%fused_computation.6 | convolution fusion | flops 6488064 | bytes 2224640 | tf_op jit(solution)/shard_map/bkl,bk->bl/dot_general | solution.py:57
  46.2 0.9 scatter_custom_fusion
  47.1 37.0 %all-reduce = f32[64,128]{1,0:T(8,128)S(1)} all-reduce(f32[64,128]{1,0:T(8,128)S(1)} %scatter_custom_fusion), channel_id=2, replica_groups=mesh['grp'=2,'blk'=8,'sub'=2] {'blk'}, use_global_device_ids=true, to_apply=%region_1.2.clone | all-reduce | flops 8192 | bytes 65536
  84.2 2.5 %psum.14 = f32[1024]{0:T(1024)S(1)} all-reduce(f32[1024]{0:T(1024)S(1)} %bitcast.81), channel_id=1, replica_groups=mesh['grp'=2,'blk'=8,'sub'=2] {'sub'}, use_global_device_ids=true, to_apply=%region_2.3 | all-reduce | flops 1024 | bytes 8192 | tf_op jit(solution)/shard_map/psum | solution.py:62
  86.6 0.0 copy-done.2
  86.6 0.0 copy-done.3
  86.6 0.0 copy-done.4
  86.7 0.0 copy-done.5
  86.7 0.0 copy-done.6
  86.7 0.0 copy-done.7
  86.7 0.6 multiply_add_fusion
  87.3 0.0 copy-done.1
  87.3 0.5 fusion.21
  87.8 30.4 %all_gather.7 = f32[64,128]{1,0:T(8,128)S(1)} all-gather(f32[8,128]{1,0:T(8,128)S(1)} %exponential_bitcast_fusion.1), channel_id=1, replica_groups=mesh['grp'=2,'blk'=8,'sub'=2] {'blk'}, dimensions={0}, use_global_device_ids=true | all-gather | bytes 36864 | tf_op jit(solution)/shard_map/all_gather | solution.py:53
  118.3 0.6 gather_fusion.1
  118.9 5.1 %fusion.4 = f32[88,1,48]{2,1,0:T(1,128)S(1)} fusion(f32[88,128,1]{1,2,0:T(1,128)S(1)} %bitcast.72, f32[1,1,88,48,128]{4,3,2,1,0:T(8,128)} %param.22), kind=kOutput, calls=%fused_computation.8 | convolution fusion | flops 6488064 | bytes 2224640 | tf_op jit(solution)/shard_map/bkl,bl->bk/dot_general | solution.py:55
  123.9 0.1 fusion.8
  124.0 1.9 %fusion = f32[88,1,128]{2,1,0:T(1,128)S(1)} fusion(f32[88,48,1]{1,2,0:T(1,128)S(1)} %bitcast.77, f32[1,1,88,48,128]{4,3,2,1,0:T(8,128)S(1)} %copy-done), kind=kOutput, calls=%fused_computation.4 | convolution fusion | flops 6488064 | bytes 2224640 | tf_op jit(solution)/shard_map/bkl,bk->bl/dot_general | solution.py:57
  125.9 0.9 scatter_custom_fusion.1
  126.8 33.0 %all-reduce.1 = f32[64,128]{1,0:T(8,128)S(1)} all-reduce(f32[64,128]{1,0:T(8,128)S(1)} %scatter_custom_fusion.1), channel_id=3, replica_groups=mesh['grp'=2,'blk'=8,'sub'=2] {'blk'}, use_global_device_ids=true, to_apply=%region_4.5.clone | all-reduce | flops 8192 | bytes 65536
  159.9 2.5 %psum.15 = f32[1024]{0:T(1024)S(1)} all-reduce(f32[1024]{0:T(1024)S(1)} %bitcast.80), channel_id=1, replica_groups=mesh['grp'=2,'blk'=8,'sub'=2] {'sub'}, use_global_device_ids=true, to_apply=%region_5.6 | all-reduce | flops 1024 | bytes 8192 | tf_op jit(solution)/shard_map/psum | solution.py:62
  162.3 0.6 multiply_add_fusion.1
  (8 shorter events, 0.1 us)
Async XLA Ops:
  0.6 43.7 %copy-start = (f32[1,1,88,48,128]{4,3,2,1,0:T(8,128)S(1)}, f32[1,1,88,48,128]{4,3,2,1,0:T(8,128)}, u32[]{:S(2)}) copy-start(f32[1,1,88,48,128]{4,3,2,1,0:T(8,128)} %param.23) | copy-start | bytes 6488068
  0.6 43.6 %copy-start.8 = (s32[1,1,88]{2,1,0:T(1,128)S(1)}, s32[1,1,88]{2,1,0:T(1,128)}, u32[]{:S(2)}) copy-start(s32[1,1,88]{2,1,0:T(1,128)} %param.21) | copy-start | bytes 1060
  39.0 47.6 %copy-start.2 = (f32[1024]{0:T(1024)S(1)}, f32[1024]{0:T(1024)}, u32[]{:S(2)}) copy-start(f32[1024]{0:T(1024)} %param.12) | copy-start | bytes 12292
  39.0 47.6 %copy-start.3 = (f32[1024]{0:T(1024)S(1)}, f32[1024]{0:T(1024)}, u32[]{:S(2)}) copy-start(f32[1024]{0:T(1024)} %param.15) | copy-start | bytes 12292
  39.0 47.6 %copy-start.4 = (f32[1024]{0:T(1024)S(1)}, f32[1024]{0:T(1024)}, u32[]{:S(2)}) copy-start(f32[1024]{0:T(1024)} %param.16) | copy-start | bytes 12292
  39.1 47.6 %copy-start.5 = (f32[1024]{0:T(1024)S(1)}, f32[1024]{0:T(1024)}, u32[]{:S(2)}) copy-start(f32[1024]{0:T(1024)} %param.14) | copy-start | bytes 12292
  39.1 47.6 %copy-start.6 = (f32[1024]{0:T(1024)S(1)}, f32[1024]{0:T(1024)}, u32[]{:S(2)}) copy-start(f32[1024]{0:T(1024)} %param.13) | copy-start | bytes 12292
  39.1 47.6 %copy-start.7 = (f32[1024]{0:T(1024)S(1)}, f32[1024]{0:T(1024)}, u32[]{:S(2)}) copy-start(f32[1024]{0:T(1024)} %param.17) | copy-start | bytes 12292
  39.1 48.2 %copy-start.1 = (f32[4,128,128]{2,1,0:T(8,128)S(1)}, f32[4,128,128]{2,1,0:T(8,128)}, u32[]{:S(2)}) copy-start(f32[4,128,128]{2,1,0:T(8,128)} %param.18) | copy-start | bytes 786436
where the time goes:
time: 163 us
  blocking collectives  138 us (85%)
  matrix products  15.9 us (10%)
  other arithmetic  4.58 us (3%)
  local copies, waits for them, and re-layouts  3.39 us (2%)
    unnamed x2, blocking collectives  70.1 us
    all_gather x2, blocking collectives, traction_of(): gathered = lax.all_gather(slip_rate, 'blk', axis=0, tiled=True)  62.6 us
    dot_general x2, matrix products, traction_of(): jnp.einsum('bkl,bl->bk', column_factor, block_input, precision=precise)  10.1 us
    psum x2, blocking collectives, traction_of(): summed = lax.psum(near_part + far_part, 'sub')  4.94 us
    dot_general x2, matrix products, traction_of(): jnp.einsum('bkl,bk->bl', row_local, coefficient, precision=precise)  3.8 us

commit v1 on v0

v1 whole, which is shorter than its diff:
```python
import functools

import jax
import jax.numpy as jnp
from jax import lax
from jax.experimental import pallas as pl
from jax.experimental.pallas import tpu as pltpu
from jax.sharding import PartitionSpec as P

damping = 0.5
time_step = 0.25
precise = lax.Precision.HIGHEST


def swap_cores(x):
    return lax.ppermute(x, "sub", [(0, 1), (1, 0)])


def swap_owners(x, bit):
    owners = lax.axis_size("blk")
    pairs = [(2 * c + s, 2 * (c ^ bit) + 1 - s) for c in range(owners) for s in range(2)]
    return lax.ppermute(x, ("blk", "sub"), pairs)


def run_copies(pairs, sems):
    copies = [pltpu.make_async_copy(source, target, sems.at[i]) for i, (source, target) in enumerate(pairs)]
    for copy in copies:
        copy.start()
    for copy in copies:
        copy.wait()


def pieces_of(source, target):
    count = source.shape[0]
    parts = next(n for n in (8, 4, 2, 1) if count % n == 0)
    step = count // parts
    return [(source.at[pl.ds(i * step, step)], target.at[pl.ds(i * step, step)]) for i in range(parts)]


def columns_kernel(source, own, target, own_copy, flags, sems):
    run_copies(pieces_of(source, target) + [(own, own_copy)], sems)
    bit = lax.broadcasted_iota(jnp.int32, flags.shape, 0)
    flags[...] = lax.shift_right_logical(lax.axis_index("blk"), bit) & 1


def rows_kernel(source, own, target, own_copy, sems):
    run_copies(pieces_of(source, target), sems)
    own_copy[...] = own[...]


def table_kernel(
    columns_all, rows_all, ranks, near_source, log_rate, log_state, load, a_sigma, b_sigma, log_dc, own,
    columns, own_ranks, place, near, a_copy, lift, own_copy,
    rows, log_rate_in, log_state_in, load_in, b_in, dc_in, sems,
):
    device = lax.axis_index("blk")
    run_copies(
        pieces_of(near_source, near)
        + [
            (columns_all.at[device], columns),
            (ranks.at[0], own_ranks),
            (rows_all.at[device], rows),
            (log_rate, log_rate_in),
            (log_state, log_state_in),
            (load, load_in),
            (a_sigma, a_copy),
            (b_sigma, b_in),
            (log_dc, dc_in),
        ],
        sems,
    )
    own_copy[...] = own[...]
    cluster = lax.broadcasted_iota(jnp.int32, place.shape, 0)
    place[...] = jnp.where(cluster == rows[...], 1.0, 0.0)
    log_values = log_rate_in[...]
    state_rate = jnp.exp(-log_state_in[...]) - jnp.exp(log_values - dc_in[...])
    inverse = (a_copy[...] + damping * jnp.exp(log_values)) * (1.0 / time_step)
    lift[...] = b_in[...] * state_rate - load_in[...] - log_values * inverse


def traction_terms(v_ref, near_start, columns, ranks, place, near, column_factor, row_factor, out, terms):
    leaf = out.shape[1]
    blocks, kmax, _ = column_factor.shape
    near_count = near.shape[0]
    sublane = lax.broadcasted_iota(jnp.int32, (8, 1), 0)

    for b in range(blocks):
        v = v_ref[pl.ds(columns[0, b], 1), :]
        rank = ranks[0, b]
        total = None
        for j in range(0, kmax, 8):
            at = pl.ds(j, 8)
            q = jnp.sum(column_factor[b, at, :] * v, axis=1, keepdims=True)
            q = jnp.where(sublane < rank - j, q, 0.0)
            piece = row_factor[b, at, :] * q
            total = piece if total is None else total + piece
        terms[pl.ds(b, 1), :] = jnp.sum(total, axis=0, keepdims=True)
    out[...] = jnp.dot(
        place[...], terms[...], precision=precise, preferred_element_type=jnp.float32
    )

    lanes = lax.broadcasted_iota(jnp.int32, (leaf, leaf), 1)
    down = lax.broadcasted_iota(jnp.int32, (leaf, leaf), 0)
    for c in range(near_count):
        here = pl.ds(near_start + c, 1)
        total = jnp.sum(near[c] * v_ref[here, :], axis=1, keepdims=True)
        out[here, :] += jnp.sum(jnp.where(lanes == down, total, 0.0), axis=0, keepdims=True)


def near_start_of(near):
    return (2 * lax.axis_index("blk") + lax.axis_index("sub")) * near.shape[0]


def first_kernel(columns, ranks, log_rate, lift, place, near, column_factor, row_factor, out, rate, terms):
    rate[...] = jnp.exp(log_rate[...])
    traction_terms(
        rate, near_start_of(near), columns, ranks, place, near, column_factor, row_factor, out, terms
    )
    per_device = lift.shape[0]
    here = pl.ds(per_device * lax.axis_index("blk"), per_device)
    out[here, :] += jnp.where(lax.axis_index("sub") == 0, lift[...], 0.0)


def second_kernel(
    columns, ranks, lifted, rate_one, a_sigma, place, near, column_factor, row_factor, out, own, rate, terms
):
    mid = lifted[...] * (-time_step / (a_sigma[...] + damping * rate_one[...]))
    rate[...] = mid
    per_device = own.shape[0]
    own[...] = rate[pl.ds(per_device * lax.axis_index("blk"), per_device), :]
    rate[...] = jnp.exp(mid)
    traction_terms(
        rate, near_start_of(near), columns, ranks, place, near, column_factor, row_factor, out, terms
    )


def shards(
    log_rate,
    log_state,
    load,
    a_sigma,
    b_sigma,
    log_dc,
    near_field,
    col_cluster,
    row_cluster,
    ranks,
    col_factor,
    row_factor,
):
    owners = lax.axis_size("blk")
    leaf = near_field.shape[1]
    per_device = log_rate.shape[0] // leaf
    clusters = owners * per_device
    blocks = col_factor.shape[2]
    depth = (owners - 1).bit_length()
    per_own = (per_device, leaf)
    log_rate, log_state, load, a_sigma, b_sigma, log_dc = (
        x.reshape(per_own) for x in (log_rate, log_state, load, a_sigma, b_sigma, log_dc)
    )

    def bit_of(axis):
        return 1 << (depth - 1 - axis)

    def set_in(axis):
        return flags[depth - 1 - axis] != 0

    def joined(axis, own, other):
        first, second = jnp.where(set_in(axis), other, own), jnp.where(set_in(axis), own, other)
        return jnp.concatenate([first, second], axis=axis)

    def flat(x):
        return x.reshape(-1, leaf)

    hbm = pl.BlockSpec(memory_space=pltpu.HBM)
    vmem = pl.BlockSpec(memory_space=pltpu.VMEM)
    smem = pl.BlockSpec(memory_space=pltpu.SMEM)
    limits = pltpu.CompilerParams(vmem_limit_bytes=8 << 20)

    def in_vmem(*shape):
        return pltpu.VMEM(shape, jnp.float32)

    def in_smem(*shape):
        return pltpu.SMEM(shape, jnp.int32)

    def in_hbm(x):
        return pltpu.with_memory_space_constraint(x, pltpu.HBM)

    def hold_factor(kernel, factor, own, own_space, more, name):
        return pl.pallas_call(
            kernel,
            out_shape=(in_vmem(*factor.shape), in_vmem(*own.shape)) + more,
            in_specs=[hbm, own_space],
            out_specs=(vmem,) * (2 + len(more)),
            scratch_shapes=[pltpu.SemaphoreType.DMA((9,))],
            compiler_params=limits,
            cost_estimate=pl.CostEstimate(flops=0, bytes_accessed=8 * factor.size, transcendentals=0),
            name=name,
        )(in_hbm(factor), own)

    def hold_tables(own):
        return pl.pallas_call(
            table_kernel,
            out_shape=(
                in_smem(1, blocks),
                in_smem(1, blocks),
                in_vmem(clusters, blocks),
                in_vmem(*near_field.shape),
                in_vmem(*per_own),
                in_vmem(*per_own),
                in_vmem(*own.shape),
            ),
            in_specs=[hbm] * 10 + [vmem],
            out_specs=(smem, smem) + (vmem,) * 5,
            scratch_shapes=[pltpu.VMEM((1, blocks), jnp.int32)]
            + [in_vmem(*per_own)] * 5
            + [pltpu.SemaphoreType.DMA((17,))],
            compiler_params=limits,
            cost_estimate=pl.CostEstimate(flops=0, bytes_accessed=8 << 20, transcendentals=0),
            name="hold_tables",
        )(
            *(
                in_hbm(x)
                for x in (
                    col_cluster, row_cluster, ranks, near_field,
                    log_rate, log_state, load, a_sigma, b_sigma, log_dc,
                )
            ),
            own,
        )

    rates = log_rate
    held = []
    for axis in range(depth):
        other = swap_owners(rates, bit_of(axis))
        if axis == 0:
            flag_shape = pltpu.VMEM((depth,) + per_own, jnp.int32)
            column_factor, rates, flags = hold_factor(
                columns_kernel, col_factor[0, 0], in_hbm(rates), hbm, (flag_shape,), "hold_columns"
            )
        elif axis == 1:
            row_local, rates = hold_factor(rows_kernel, row_factor[0, 0], rates, vmem, (), "hold_rows")
        elif axis == 2:
            columns, own_ranks, place, near, own_a, lift, rates = hold_tables(rates)
        shape = (2,) * axis + (1,) * (depth - axis) + per_own
        rates = flat(joined(axis, rates.reshape(shape), other.reshape(shape)))

    blocks_and_near = (place, near, column_factor, row_local)
    term_scratch = in_vmem(blocks, leaf)
    part, rate_one = pl.pallas_call(
        first_kernel,
        out_shape=(in_vmem(clusters, leaf), in_vmem(clusters, leaf)),
        in_specs=[smem, smem] + [vmem] * 6,
        out_specs=(vmem, vmem),
        scratch_shapes=[term_scratch],
        compiler_params=limits,
        name="section_one",
    )(columns, own_ranks, rates, lift, *blocks_and_near)

    part = part + swap_cores(part)
    all_a = own_a
    for axis in range(depth):
        other = swap_owners(jnp.concatenate([part, all_a], axis=0), bit_of(axis))
        part = part + other[:clusters]
        shape = (2,) * axis + (1,) * (depth - axis) + per_own
        all_a = flat(joined(axis, all_a.reshape(shape), other[clusters:].reshape(shape)))

    part, mid_rate = pl.pallas_call(
        second_kernel,
        out_shape=(in_vmem(clusters, leaf), in_vmem(*per_own)),
        in_specs=[smem, smem] + [vmem] * 7,
        out_specs=(vmem, vmem),
        scratch_shapes=[in_vmem(clusters, leaf), term_scratch],
        compiler_params=limits,
        name="section_two",
    )(columns, own_ranks, part, rate_one, all_a, *blocks_and_near)

    state_one = jnp.exp(-log_state) - jnp.exp(log_rate - log_dc)
    mid_state = log_state + time_step * state_one
    state_two = jnp.exp(-mid_state) - jnp.exp(mid_rate - log_dc)
    gain_two = 0.5 * time_step / (a_sigma + damping * jnp.exp(mid_rate))
    base_two = 0.5 * (log_rate + mid_rate) + gain_two * (load - b_sigma * state_two)
    new_log_state = log_state + 0.5 * time_step * (state_one + state_two)

    part = part.reshape((2,) * depth + per_own)
    for axis in reversed(range(depth)):
        low = lax.slice_in_dim(part, 0, 1, axis=axis)
        high = lax.slice_in_dim(part, 1, 2, axis=axis)
        send = jnp.where(set_in(axis), low, high)
        keep = jnp.where(set_in(axis), high, low)
        part = keep + swap_owners(flat(send), bit_of(axis)).reshape(keep.shape)
    part = part.reshape(per_own)
    part = part + swap_cores(part)
    new_log_rate = base_two - gain_two * part
    return (new_log_rate.reshape(-1), new_log_state.reshape(-1))


def solution(mesh):
    placed = (
        P(("grp", "blk")),
        P(("grp", "blk")),
        P(("grp", "blk")),
        P(("grp", "blk")),
        P(("grp", "blk")),
        P(("grp", "blk")),
        P(("blk", "sub"), None, None),
        P(None, "sub", None),
        P(None, "sub", None),
        P("blk", "sub", None),
        P("blk", "sub", None, None, None),
        P("blk", "sub", None, None, None),
    )
    return jax.shard_map(
        shards,
        mesh=mesh,
        in_specs=placed,
        out_specs=(P(("grp", "blk")), P(("grp", "blk"))),
        check_vma=False,
    )
```

time: 163 us -> 40.8 us (0.25)
  blocking collectives: 138 us -> 0 us
  starting transfers between devices: 0 us -> 19.9 us
  matrix products: 15.9 us -> 0 us
  waiting for transfers between devices: 0 us -> 12.9 us
  Pallas kernels: 0 us -> 6.04 us
  other arithmetic: 4.58 us -> 0.79 us
  local copies, waits for them, and re-layouts: 3.39 us -> 0.06 us
    unnamed x2 -> x0, blocking collectives: 70.1 us -> none
    all_gather x2 -> x0, blocking collectives: 62.6 us -> none  [traction_of(): gathered = lax.all_gather(slip_rate, 'blk', axis=0, tiled=True)]
    ppermute x0 -> x11, starting transfers between devices: none -> 19.9 us  [the longest x9 19.4 us: swap_owners(): return lax.ppermute(x, ('blk', 'sub'), pairs)]
    dot_general x6 -> x0, matrix products: 15.9 us -> none  [the longest x2 10.1 us: traction_of(): jnp.einsum('bkl,bl->bk', column_factor, block_input, precision=precise)]
    ppermute x0 -> x11, waiting for transfers between devices: none -> 12.9 us  [the longest x9 11 us: swap_owners(): return lax.ppermute(x, ('blk', 'sub'), pairs)]
    pallas_call x0 -> x5, Pallas kernels: none -> 6.04 us  [the longest x2 3.2 us: hold_factor(): pl.pallas_call(kernel, out_shape=(in_vmem(*factor.shape), in_vmem(*own.sh...]
    psum x2 -> x0, blocking collectives: 4.94 us -> none  [traction_of(): summed = lax.psum(near_part + far_part, 'sub')]
    scatter-add x2 -> x0, other arithmetic: 1.8 us -> none  [traction_of(): jnp.zeros((owners * per_device, leaf), jnp.float32).at[own_rows]]
  transfers between devices with their start and end apart: 0 -> 11, of which waited for: 0 -> 9; matrix products, arithmetic and copies ran while one was open for 0% -> 0% of each run, Pallas kernels for 0% -> 11%
where the time goes in v1:
time: 40.8 us; the launch traced here: 40.6 us
  starting transfers between devices  19.9 us (49%)
  waiting for transfers between devices  12.9 us (32%)
  Pallas kernels  6.04 us (15%)
  between operations  0.89 us (2%)
  other arithmetic  0.79 us (2%)
    ppermute x9, starting transfers between devices, swap_owners(): return lax.ppermute(x, ('blk', 'sub'), pairs)  19.4 us
    ppermute x9, waiting for transfers between devices, swap_owners(): return lax.ppermute(x, ('blk', 'sub'), pairs)  11 us
    pallas_call x2, Pallas kernels, hold_factor(): pl.pallas_call(kernel, out_shape=(in_vmem(*factor.shape), in_vmem(*own.sh...  3.2 us
    ppermute x2, waiting for transfers between devices, swap_cores(): return lax.ppermute(x, 'sub', [(0, 1), (1, 0)])  1.94 us
    pallas_call x1, Pallas kernels, hold_tables(): pl.pallas_call(table_kernel, out_shape=(in_smem(1, blocks), in_smem(1, bl...  1.13 us
    pallas_call x1, Pallas kernels, shards(): pl.pallas_call(second_kernel, out_shape=(in_vmem(clusters, leaf), in_vmem...  0.86 us
    pallas_call x1, Pallas kernels, shards(): pl.pallas_call(first_kernel, out_shape=(in_vmem(clusters, leaf), in_vmem(...  0.85 us
  transfers between devices with their start and end apart: 11, of which 9 were waited for; matrix products, arithmetic and copies ran while one was open for 0% of the time, Pallas kernels for 11%

profile of v1, /device:TPU:0, one launch (start us, length us, event | category | flops | bytes accessed | tf_op | source)
XLA Modules:
  0.0 40.6 jit_solution(2418407817191976626)
XLA Ops:
  0.6 3.5 %collective-permute-start = (f32[8,128]{1,0:T(8,128)}, f32[8,128]{1,0:T(8,128)S(1)}, u32[]{:S(2)}, u32[]{:S(2)}) collective-permute-start(f32[8,128]{1,0:T(8,128)} %bitcast.140), channel_id=1, source_target_pairs={{0,9},{1,8},{2,11},{3,10},{4,13},{5,12},{6,15},{7,14},{8,1},{9,0},... | collective-permute-start | bytes 12296 | tf_op jit(solution)/shard_map/ppermute | solution.py:22
  4.2 1.6 %hold_columns.1 = (f32[88,48,128]{2,1,0:T(8,128)S(1)}, f32[8,128]{1,0:T(8,128)S(1)}, s32[3,8,128]{2,1,0:T(8,128)S(1)}) custom-call(f32[88,48,128]{2,1,0:T(8,128)} %bitcast.136, f32[8,128]{1,0:T(8,128)} %bitcast.141), custom_call_target="tpu_custom_call" | custom-call | bytes 4325376 | tf_op jit(solution)/shard_map/hold_columns/pallas_call | solution.py:190
  5.8 0.0 collective-permute-done
  5.8 1.9 %collective-permute-start.1 = (f32[16,128]{1,0:T(8,128)S(1)}, f32[16,128]{1,0:T(8,128)S(1)}, u32[]{:S(2)}, u32[]{:S(2)}) collective-permute-start(f32[16,128]{1,0:T(8,128)S(1)} %maximum_bitcast_fusion.own), channel_id=1, source_target_pairs={{0,5},{1,4},{2,7},{3,6},{4,1},{5,0},{6,3},{7,2},{8,13},{9,12},{10,... | collective-permute-start | bytes 24584 | tf_op jit(solution)/shard_map/ppermute | solution.py:22
  7.8 1.6 %hold_rows.1 = (f32[88,48,128]{2,1,0:T(8,128)S(1)}, f32[16,128]{1,0:T(8,128)S(1)}) custom-call(f32[88,48,128]{2,1,0:T(8,128)} %bitcast.137, f32[16,128]{1,0:T(8,128)S(1)} %maximum_bitcast_fusion.own), custom_call_target="tpu_custom_call" | custom-call | bytes 4325376 | tf_op jit(solution)/shard_map/hold_rows/pallas_call | solution.py:190
  9.4 0.0 collective-permute-done.1
  9.4 1.5 %collective-permute-start.2 = (f32[32,128]{1,0:T(8,128)S(1)}, f32[32,128]{1,0:T(8,128)S(1)}, u32[]{:S(2)}, u32[]{:S(2)}) collective-permute-start(f32[32,128]{1,0:T(8,128)S(1)} %bitcast.132), channel_id=1, source_target_pairs={{0,3},{1,2},{2,1},{3,0},{4,7},{5,6},{6,5},{7,4},{8,11},{9,10},{10,... | collective-permute-start | bytes 49160 | tf_op jit(solution)/shard_map/ppermute | solution.py:22
  10.9 1.1 %hold_tables.1 = (s32[1,88]{1,0:T(1,128)S(4)}, s32[1,88]{1,0:T(1,128)S(4)}, f32[64,88]{1,0:T(8,128)S(1)}, f32[4,128,128]{2,1,0:T(8,128)S(1)}, f32[8,128]{1,0:T(8...) custom-call(s32[8,1,88]{2,1,0:T(1,128)} %columns_all.1, s32[8,1,88]{2,1,0:T(1,128)} %rows_all.1, ...), custom_call_target="tpu_custom_call" | custom-call | bytes 8388608 | tf_op jit(solution)/shard_map/hold_tables/pallas_call | solution.py:202
  12.0 0.6 %collective-permute-done.2 = f32[32,128]{1,0:T(8,128)S(1)} collective-permute-done((f32[32,128]{1,0:T(8,128)S(1)}, f32[32,128]{1,0:T(8,128)S(1)}, u32[]{:S(2)}, u32[]{:S(2)}) %collective-permute-start.2) | collective-permute-done | bytes 16416 | tf_op jit(solution)/shard_map/ppermute | solution.py:22
  12.7 0.9 %section_one.1 = (f32[64,128]{1,0:T(8,128)S(1)}, f32[64,128]{1,0:T(8,128)S(1)}) custom-call(s32[1,88]{1,0:T(1,128)S(4)} %get-tuple-element.21.columns, s32[1,88]{1,0:T(1,128)S(4)} %get-tuple-element.22.ranks, f32[64,128]{1,0:T(8,128)S(1)} %bitcast.131, f32[8,128]{1,0:T(8,128)S(1)} %get-tuple-element.24.lift, f32[64,88]{1,0:T(8,128)S(1)} %get-tuple-element.25.place, ...), custom_call_target="tpu_custom_call" | custom-call | tf_op jit(solution)/shard_map/section_one/pallas_call | solution.py:250
  13.5 0.4 collective-permute-start.3
  13.9 0.9 %collective-permute-done.3 = f32[64,128]{1,0:T(8,128)S(1)} collective-permute-done((f32[64,128]{1,0:T(8,128)S(1)}, f32[64,128]{1,0:T(8,128)S(1)}, u32[]{:S(2)}, u32[]{:S(2)}) %collective-permute-start.3) | collective-permute-done | bytes 32800 | tf_op jit(solution)/shard_map/ppermute | solution.py:16
  14.8 2.6 %collective-permute-start.4 = (f32[72,128]{1,0:T(8,128)S(1)}, f32[72,128]{1,0:T(8,128)S(1)}, u32[]{:S(2)}, u32[]{:S(2)}) collective-permute-start(f32[72,128]{1,0:T(8,128)S(1)} %pad_maximum_fusion.2), channel_id=1, source_target_pairs={{0,9},{1,8},{2,11},{3,10},{4,13},{5,12},{6,15},{7,14},{8,1},{9,0},... | collective-permute-start | bytes 110600 | tf_op jit(solution)/shard_map/ppermute | solution.py:22
  17.4 1.8 %collective-permute-done.4 = f32[72,128]{1,0:T(8,128)S(1)} collective-permute-done((f32[72,128]{1,0:T(8,128)S(1)}, f32[72,128]{1,0:T(8,128)S(1)}, u32[]{:S(2)}, u32[]{:S(2)}) %collective-permute-start.4) | collective-permute-done | bytes 36896 | tf_op jit(solution)/shard_map/ppermute | solution.py:22
  19.2 1.5 %collective-permute-start.5 = (f32[80,128]{1,0:T(8,128)S(1)}, f32[80,128]{1,0:T(8,128)S(1)}, u32[]{:S(2)}, u32[]{:S(2)}) collective-permute-start(f32[80,128]{1,0:T(8,128)S(1)} %pad_maximum_fusion.1), channel_id=1, source_target_pairs={{0,5},{1,4},{2,7},{3,6},{4,1},{5,0},{6,3},{7,2},{8,13},{9,12},{10,... | collective-permute-start | bytes 122888 | tf_op jit(solution)/shard_map/ppermute | solution.py:22
  20.7 2.0 %collective-permute-done.5 = f32[80,128]{1,0:T(8,128)S(1)} collective-permute-done((f32[80,128]{1,0:T(8,128)S(1)}, f32[80,128]{1,0:T(8,128)S(1)}, u32[]{:S(2)}, u32[]{:S(2)}) %collective-permute-start.5) | collective-permute-done | bytes 40992 | tf_op jit(solution)/shard_map/ppermute | solution.py:22
  22.7 1.5 %collective-permute-start.6 = (f32[96,128]{1,0:T(8,128)S(1)}, f32[96,128]{1,0:T(8,128)S(1)}, u32[]{:S(2)}, u32[]{:S(2)}) collective-permute-start(f32[96,128]{1,0:T(8,128)S(1)} %pad_maximum_fusion), channel_id=1, source_target_pairs={{0,3},{1,2},{2,1},{3,0},{4,7},{5,6},{6,5},{7,4},{8,11},{9,10},{10,... | collective-permute-start | bytes 147464 | tf_op jit(solution)/shard_map/ppermute | solution.py:22
  24.2 2.2 %collective-permute-done.6 = f32[96,128]{1,0:T(8,128)S(1)} collective-permute-done((f32[96,128]{1,0:T(8,128)S(1)}, f32[96,128]{1,0:T(8,128)S(1)}, u32[]{:S(2)}, u32[]{:S(2)}) %collective-permute-start.6) | collective-permute-done | bytes 49184 | tf_op jit(solution)/shard_map/ppermute | solution.py:22
  26.4 0.0 copy-start
  26.4 0.0 copy-start.1
  26.5 0.0 copy-start.2
  26.5 0.0 copy-start.3
  26.5 0.0 copy-start.4
  26.5 0.0 copy-start.5
  26.5 0.9 %section_two.1 = (f32[64,128]{1,0:T(8,128)S(1)}, f32[8,128]{1,0:T(8,128)S(1)}) custom-call(s32[1,88]{1,0:T(1,128)S(4)} %get-tuple-element.21.columns, s32[1,88]{1,0:T(1,128)S(4)} %get-tuple-element.22.ranks, f32[64,128]{1,0:T(8,128)S(1)} %slice_add_fusion.lifted, f32[64,128]{1,0:T(8,128)S(1)} %get-tuple-element.31.rate_one, f32[64,128]{1,0:T(8,128)S(1)} %bitcast.130, ...), custom_call_target="tpu_custom_call" | custom-call | tf_op jit(solution)/shard_map/section_two/pallas_call | solution.py:268
  27.4 1.5 %collective-permute-start.7 = (f32[32,128]{1,0:T(8,128)S(1)}, f32[32,128]{1,0:T(8,128)S(1)}, u32[]{:S(2)}, u32[]{:S(2)}) collective-permute-start(f32[32,128]{1,0:T(8,128)S(1)} %bitcast.148), channel_id=1, source_target_pairs={{0,3},{1,2},{2,1},{3,0},{4,7},{5,6},{6,5},{7,4},{8,11},{9,10},{10,... | collective-permute-start | bytes 49160 | tf_op jit(solution)/shard_map/ppermute | solution.py:22
  28.9 1.8 %collective-permute-done.7 = f32[32,128]{1,0:T(8,128)S(1)} collective-permute-done((f32[32,128]{1,0:T(8,128)S(1)}, f32[32,128]{1,0:T(8,128)S(1)}, u32[]{:S(2)}, u32[]{:S(2)}) %collective-permute-start.7) | collective-permute-done | bytes 16416 | tf_op jit(solution)/shard_map/ppermute | solution.py:22
  30.7 2.2 %collective-permute-start.8 = (f32[16,128]{1,0:T(8,128)S(1)}, f32[16,128]{1,0:T(8,128)S(1)}, u32[]{:S(2)}, u32[]{:S(2)}) collective-permute-start(f32[16,128]{1,0:T(8,128)S(1)} %fusion.1), channel_id=1, source_target_pairs={{0,5},{1,4},{2,7},{3,6},{4,1},{5,0},{6,3},{7,2},{8,13},{9,12},{10,... | collective-permute-start | bytes 24584 | tf_op jit(solution)/shard_map/ppermute | solution.py:22
  32.9 1.4 %collective-permute-done.8 = f32[16,128]{1,0:T(8,128)S(1)} collective-permute-done((f32[16,128]{1,0:T(8,128)S(1)}, f32[16,128]{1,0:T(8,128)S(1)}, u32[]{:S(2)}, u32[]{:S(2)}) %collective-permute-start.8) | collective-permute-done | bytes 8224 | tf_op jit(solution)/shard_map/ppermute | solution.py:22
  34.3 3.1 %collective-permute-start.9 = (f32[8,128]{1,0:T(8,128)S(1)}, f32[8,128]{1,0:T(8,128)S(1)}, u32[]{:S(2)}, u32[]{:S(2)}) collective-permute-start(f32[8,128]{1,0:T(8,128)S(1)} %fusion.6), channel_id=1, source_target_pairs={{0,9},{1,8},{2,11},{3,10},{4,13},{5,12},{6,15},{7,14},{8,1},{9,0},... | collective-permute-start | bytes 12296 | tf_op jit(solution)/shard_map/ppermute | solution.py:22
  37.4 1.3 %collective-permute-done.9 = f32[8,128]{1,0:T(8,128)S(1)} collective-permute-done((f32[8,128]{1,0:T(8,128)S(1)}, f32[8,128]{1,0:T(8,128)S(1)}, u32[]{:S(2)}, u32[]{:S(2)}) %collective-permute-start.9) | collective-permute-done | bytes 4128 | tf_op jit(solution)/shard_map/ppermute | solution.py:22
  38.7 0.1 collective-permute-start.10
  38.9 1.0 %collective-permute-done.10 = f32[8,128]{1,0:T(8,128)S(1)} collective-permute-done((f32[8,128]{1,0:T(8,128)S(1)}, f32[8,128]{1,0:T(8,128)S(1)}, u32[]{:S(2)}, u32[]{:S(2)}) %collective-permute-start.10) | collective-permute-done | bytes 4128 | tf_op jit(solution)/shard_map/ppermute | solution.py:16
  39.9 0.0 copy-done
  39.9 0.0 copy-done.1
  39.9 0.0 copy-done.2
  39.9 0.0 copy-done.3
  39.9 0.0 copy-done.4
  39.9 0.0 copy-done.5
  39.9 0.6 %add_bitcast_fusion = (f32[1024]{0:T(1024)}, f32[1024]{0:T(1024)}) fusion(f32[8,128]{1,0:T(8,128)S(1)} %get-tuple-element.32, f32[1024]{0:T(1024)S(1)} %copy-done.5, f32[1024]{0:T(1024)S(1)} %copy-done.1, f32[1024]{0:T(1024)S(1)} %copy-done, f32[8,128]{1,0:T(8,128)S(1)} %fusion.5, f32[8,128]{1,0:T(8,128)S(1)} %collective-permute-done.10, ...), kind=kLoop, calls=%fused_computation.38 | loop fusion | flops 23552 | bytes 45056 | tf_op jit(solution)/shard_map/reshape | solution.py:295
  (35 shorter events, 0.2 us)
Async XLA Ops:
  0.6 5.2 %collective-permute-start = (f32[8,128]{1,0:T(8,128)}, f32[8,128]{1,0:T(8,128)S(1)}, u32[]{:S(2)}, u32[]{:S(2)}) collective-permute-start(f32[8,128]{1,0:T(8,128)} %bitcast.140), channel_id=1, source_target_pairs={{0,9},{1,8},{2,11},{3,10},{4,13},{5,12},{6,15},{7,14},{8,1},{9,0},... | collective-permute-start | bytes 12296 | tf_op jit(solution)/shard_map/ppermute | solution.py:22
  5.8 3.5 %collective-permute-start.1 = (f32[16,128]{1,0:T(8,128)S(1)}, f32[16,128]{1,0:T(8,128)S(1)}, u32[]{:S(2)}, u32[]{:S(2)}) collective-permute-start(f32[16,128]{1,0:T(8,128)S(1)} %maximum_bitcast_fusion.own), channel_id=1, source_target_pairs={{0,5},{1,4},{2,7},{3,6},{4,1},{5,0},{6,3},{7,2},{8,13},{9,12},{10,... | collective-permute-start | bytes 24584 | tf_op jit(solution)/shard_map/ppermute | solution.py:22
  9.4 3.2 %collective-permute-start.2 = (f32[32,128]{1,0:T(8,128)S(1)}, f32[32,128]{1,0:T(8,128)S(1)}, u32[]{:S(2)}, u32[]{:S(2)}) collective-permute-start(f32[32,128]{1,0:T(8,128)S(1)} %bitcast.132), channel_id=1, source_target_pairs={{0,3},{1,2},{2,1},{3,0},{4,7},{5,6},{6,5},{7,4},{8,11},{9,10},{10,... | collective-permute-start | bytes 49160 | tf_op jit(solution)/shard_map/ppermute | solution.py:22
  13.5 1.3 %collective-permute-start.3 = (f32[64,128]{1,0:T(8,128)S(1)}, f32[64,128]{1,0:T(8,128)S(1)}, u32[]{:S(2)}, u32[]{:S(2)}) collective-permute-start(f32[64,128]{1,0:T(8,128)S(1)} %get-tuple-element.29), channel_id=1, source_target_pairs={{0,1},{1,0},{2,3},{3,2},{4,5},{5,4},{6,7},{7,6},{8,9},{9,8},{10,11... | collective-permute-start | bytes 98312 | tf_op jit(solution)/shard_map/ppermute | solution.py:16
  14.8 4.3 %collective-permute-start.4 = (f32[72,128]{1,0:T(8,128)S(1)}, f32[72,128]{1,0:T(8,128)S(1)}, u32[]{:S(2)}, u32[]{:S(2)}) collective-permute-start(f32[72,128]{1,0:T(8,128)S(1)} %pad_maximum_fusion.2), channel_id=1, source_target_pairs={{0,9},{1,8},{2,11},{3,10},{4,13},{5,12},{6,15},{7,14},{8,1},{9,0},... | collective-permute-start | bytes 110600 | tf_op jit(solution)/shard_map/ppermute | solution.py:22
  19.2 3.5 %collective-permute-start.5 = (f32[80,128]{1,0:T(8,128)S(1)}, f32[80,128]{1,0:T(8,128)S(1)}, u32[]{:S(2)}, u32[]{:S(2)}) collective-permute-start(f32[80,128]{1,0:T(8,128)S(1)} %pad_maximum_fusion.1), channel_id=1, source_target_pairs={{0,5},{1,4},{2,7},{3,6},{4,1},{5,0},{6,3},{7,2},{8,13},{9,12},{10,... | collective-permute-start | bytes 122888 | tf_op jit(solution)/shard_map/ppermute | solution.py:22
  22.7 3.7 %collective-permute-start.6 = (f32[96,128]{1,0:T(8,128)S(1)}, f32[96,128]{1,0:T(8,128)S(1)}, u32[]{:S(2)}, u32[]{:S(2)}) collective-permute-start(f32[96,128]{1,0:T(8,128)S(1)} %pad_maximum_fusion), channel_id=1, source_target_pairs={{0,3},{1,2},{2,1},{3,0},{4,7},{5,6},{6,5},{7,4},{8,11},{9,10},{10,... | collective-permute-start | bytes 147464 | tf_op jit(solution)/shard_map/ppermute | solution.py:22
  26.4 13.5 %copy-start = (f32[1024]{0:T(1024)S(1)}, f32[1024]{0:T(1024)}, u32[]{:S(2)}) copy-start(f32[1024]{0:T(1024)} %param.12) | copy-start | bytes 12292
  26.4 13.5 %copy-start.1 = (f32[1024]{0:T(1024)S(1)}, f32[1024]{0:T(1024)}, u32[]{:S(2)}) copy-start(f32[1024]{0:T(1024)} %param.13) | copy-start | bytes 12292
  26.5 13.5 %copy-start.2 = (f32[1024]{0:T(1024)S(1)}, f32[1024]{0:T(1024)}, u32[]{:S(2)}) copy-start(f32[1024]{0:T(1024)} %param.14) | copy-start | bytes 12292
  26.5 13.4 %copy-start.3 = (f32[1024]{0:T(1024)S(1)}, f32[1024]{0:T(1024)}, u32[]{:S(2)}) copy-start(f32[1024]{0:T(1024)} %param.15) | copy-start | bytes 12292
  26.5 13.4 %copy-start.4 = (f32[1024]{0:T(1024)S(1)}, f32[1024]{0:T(1024)}, u32[]{:S(2)}) copy-start(f32[1024]{0:T(1024)} %param.16) | copy-start | bytes 12292
  26.5 13.4 %copy-start.5 = (f32[1024]{0:T(1024)S(1)}, f32[1024]{0:T(1024)}, u32[]{:S(2)}) copy-start(f32[1024]{0:T(1024)} %param.17) | copy-start | bytes 12292
  27.4 3.2 %collective-permute-start.7 = (f32[32,128]{1,0:T(8,128)S(1)}, f32[32,128]{1,0:T(8,128)S(1)}, u32[]{:S(2)}, u32[]{:S(2)}) collective-permute-start(f32[32,128]{1,0:T(8,128)S(1)} %bitcast.148), channel_id=1, source_target_pairs={{0,3},{1,2},{2,1},{3,0},{4,7},{5,6},{6,5},{7,4},{8,11},{9,10},{10,... | collective-permute-start | bytes 49160 | tf_op jit(solution)/shard_map/ppermute | solution.py:22
  30.7 3.6 %collective-permute-start.8 = (f32[16,128]{1,0:T(8,128)S(1)}, f32[16,128]{1,0:T(8,128)S(1)}, u32[]{:S(2)}, u32[]{:S(2)}) collective-permute-start(f32[16,128]{1,0:T(8,128)S(1)} %fusion.1), channel_id=1, source_target_pairs={{0,5},{1,4},{2,7},{3,6},{4,1},{5,0},{6,3},{7,2},{8,13},{9,12},{10,... | collective-permute-start | bytes 24584 | tf_op jit(solution)/shard_map/ppermute | solution.py:22
  34.3 4.5 %collective-permute-start.9 = (f32[8,128]{1,0:T(8,128)S(1)}, f32[8,128]{1,0:T(8,128)S(1)}, u32[]{:S(2)}, u32[]{:S(2)}) collective-permute-start(f32[8,128]{1,0:T(8,128)S(1)} %fusion.6), channel_id=1, source_target_pairs={{0,9},{1,8},{2,11},{3,10},{4,13},{5,12},{6,15},{7,14},{8,1},{9,0},... | collective-permute-start | bytes 12296 | tf_op jit(solution)/shard_map/ppermute | solution.py:22
  38.7 1.2 %collective-permute-start.10 = (f32[8,128]{1,0:T(8,128)S(1)}, f32[8,128]{1,0:T(8,128)S(1)}, u32[]{:S(2)}, u32[]{:S(2)}) collective-permute-start(f32[8,128]{1,0:T(8,128)S(1)} %fusion.5), channel_id=1, source_target_pairs={{0,1},{1,0},{2,3},{3,2},{4,5},{5,4},{6,7},{7,6},{8,9},{9,8},{10,11... | collective-permute-start | bytes 12296 | tf_op jit(solution)/shard_map/ppermute | solution.py:16

commit v2 on v1

v2 whole, which is shorter than its diff:
```python
import functools

import jax
import jax.numpy as jnp
from jax import lax
from jax.experimental import pallas as pl
from jax.experimental.pallas import tpu as pltpu
from jax.sharding import PartitionSpec as P

damping = 0.5
time_step = 0.25
precise = lax.Precision.HIGHEST


def swap_cores(x):
    return lax.ppermute(x, "sub", [(0, 1), (1, 0)])


def swap_owners(x, bit):
    owners = lax.axis_size("blk")
    pairs = [(2 * c + s, 2 * (c ^ bit) + 1 - s) for c in range(owners) for s in range(2)]
    return lax.ppermute(x, ("blk", "sub"), pairs)


def run_copies(pairs, sems):
    copies = [pltpu.make_async_copy(source, target, sems.at[i]) for i, (source, target) in enumerate(pairs)]
    for copy in copies:
        copy.start()
    for copy in copies:
        copy.wait()


def pieces_of(source, target, first=0):
    return [(source.at[pl.ds(first, target.shape[0])], target)]


def near_rows(v_ref, near):
    near_count, leaf, _ = near.shape
    lanes = lax.broadcasted_iota(jnp.int32, (leaf, leaf), 1)
    down = lax.broadcasted_iota(jnp.int32, (leaf, leaf), 0)
    row = lax.broadcasted_iota(jnp.int32, v_ref.shape, 0)
    first = lax.axis_index("sub") * near_count
    placed = jnp.zeros(v_ref.shape, jnp.float32)
    for c in range(near_count):
        total = jnp.sum(near[c] * v_ref[pl.ds(first + c, 1), :], axis=1, keepdims=True)
        total = jnp.sum(jnp.where(lanes == down, total, 0.0), axis=0, keepdims=True)
        placed = jnp.where(row == first + c, total, placed)
    return placed


def first_hold_kernel(
    columns_all, rows_all, ranks, near_source, factor, own,
    table, near_one, own_copy, flags, near, held,
    numbers, rate, sems,
):
    device = lax.axis_index("blk")
    run_copies(
        [
            (own, own_copy),
            (near_source, near),
            (columns_all.at[device], numbers.at[0]),
            (rows_all.at[device], numbers.at[1]),
            (ranks.at[0], numbers.at[2]),
        ]
        + pieces_of(factor, held),
        sems,
    )
    rate[...] = jnp.exp(own_copy[...])
    near_one[...] = near_rows(rate, near)
    table[...] = jnp.zeros(table.shape, jnp.float32)
    for i in range(3):
        table[pl.ds(i, 1), pl.ds(0, numbers.shape[2])] = numbers[i].astype(jnp.float32)
    bit = lax.broadcasted_iota(jnp.int32, flags.shape, 0)
    flags[...] = lax.shift_right_logical(device, bit) & 1


def second_hold_kernel(given, columns, rows, own, held_columns, held_rows, own_copy, sems):
    done = columns.shape[0] - held_columns.shape[0]
    run_copies(pieces_of(columns, held_columns, done) + pieces_of(rows, held_rows), sems)
    own_copy[...] = own[...]


def third_hold_kernel(
    done, given, given_other, factor, log_rate, log_state, load, a_sigma, b_sigma, log_dc, own,
    tables, place, held, a_copy, lift, own_copy,
    log_rate_in, log_state_in, load_in, b_in, dc_in, sems,
):
    run_copies(
        pieces_of(factor, held, done)
        + [
            (given.at[0], tables.at[0]),
            (given_other.at[0], tables.at[1]),
            (log_rate, log_rate_in),
            (log_state, log_state_in),
            (load, load_in),
            (a_sigma, a_copy),
            (b_sigma, b_in),
            (log_dc, dc_in),
        ],
        sems,
    )
    own_copy[...] = own[...]
    blocks = place.shape[2]
    cluster = lax.broadcasted_iota(jnp.int32, place.shape[1:], 0).astype(jnp.float32)
    for g, pack in enumerate((given, given_other)):
        place[g] = jnp.where(cluster == pack[0, 1:2, :blocks], 1.0, 0.0).astype(place.dtype)
    log_values = log_rate_in[...]
    state_rate = jnp.exp(-log_state_in[...]) - jnp.exp(log_values - dc_in[...])
    inverse = (a_copy[...] + damping * jnp.exp(log_values)) * (1.0 / time_step)
    lift[...] = (given[1] + given_other[1]) + (b_in[...] * state_rate - load_in[...] - log_values * inverse)


def near_kernel(mid_rate, near, out, rate):
    rate[...] = jnp.exp(mid_rate[...])
    out[...] = near_rows(rate, near)


def split_three(x):
    parts = []
    for _ in range(3):
        parts.append(x.astype(jnp.bfloat16))
        x = x - parts[-1].astype(jnp.float32)
    return parts


def section(v_ref, tables, known, out, terms):
    place, columns_a, columns_b, rows_a, rows_b, columns_other, rows_other = known
    sublane = lax.broadcasted_iota(jnp.int32, (8, 1), 0)
    summed = None
    for g, column_parts, row_parts in (
        (0, [columns_a, columns_b], [rows_a, rows_b]),
        (1, [columns_other], [rows_other]),
    ):
        column_tiles = [(part, i) for part in column_parts for i in range(part.shape[0])]
        row_tiles = [(part, i) for part in row_parts for i in range(part.shape[0])]
        for b, ((column_factor, i), (row_factor, k)) in enumerate(zip(column_tiles, row_tiles)):
            v = v_ref[pl.ds(tables[g, 0, b].astype(jnp.int32), 1), :]
            rank = tables[g, 2, b].astype(jnp.int32)
            total = None
            for j in range(0, column_factor.shape[1], 8):
                at = pl.ds(j, 8)
                q = jnp.sum(column_factor[i, at, :] * v, axis=1, keepdims=True)
                q = jnp.where(sublane < rank - j, q, 0.0)
                piece = row_factor[k, at, :] * q
                total = piece if total is None else total + piece
            terms[g, pl.ds(b, 1), :] = jnp.sum(total, axis=0, keepdims=True)
        high, middle, low = (
            jnp.dot(place[g], x, preferred_element_type=jnp.float32) for x in split_three(terms[g])
        )
        part = high + (middle + low)
        summed = part if summed is None else summed + part
    out[...] = summed


def first_kernel(tables, log_rate, lift, *refs):
    *known, out, rate, terms = refs
    rate[...] = jnp.exp(log_rate[...])
    section(rate, tables, known, out, terms)
    per_device = lift.shape[0]
    out[pl.ds(per_device * lax.axis_index("blk"), per_device), :] += lift[...]


def second_kernel(tables, lifted, rate_one, a_sigma, *refs):
    *known, out, own, rate, terms = refs
    mid = lifted[...] * (-time_step / (a_sigma[...] + damping * rate_one[...]))
    rate[...] = mid
    per_device = own.shape[0]
    own[...] = rate[pl.ds(per_device * lax.axis_index("blk"), per_device), :]
    rate[...] = jnp.exp(mid)
    section(rate, tables, known, out, terms)


def shards(
    log_rate,
    log_state,
    load,
    a_sigma,
    b_sigma,
    log_dc,
    near_field,
    col_cluster,
    row_cluster,
    ranks,
    col_factor,
    row_factor,
):
    owners = lax.axis_size("blk")
    leaf = near_field.shape[1]
    per_device = log_rate.shape[0] // leaf
    clusters = owners * per_device
    _, _, blocks, kmax, _ = col_factor.shape
    depth = (owners - 1).bit_length()
    per_own = (per_device, leaf)
    log_rate, log_state, load, a_sigma, b_sigma, log_dc = (
        x.reshape(per_own) for x in (log_rate, log_state, load, a_sigma, b_sigma, log_dc)
    )
    col_factor, row_factor = col_factor[0, 0], row_factor[0, 0]

    def bit_of(axis):
        return 1 << (depth - 1 - axis)

    def set_in(axis):
        return flags[depth - 1 - axis] != 0

    def joined(axis, own, other):
        first, second = jnp.where(set_in(axis), other, own), jnp.where(set_in(axis), own, other)
        return jnp.concatenate([first, second], axis=axis)

    def flat(x):
        return x.reshape(-1, leaf)

    hbm = pl.BlockSpec(memory_space=pltpu.HBM)
    vmem = pl.BlockSpec(memory_space=pltpu.VMEM)
    smem = pl.BlockSpec(memory_space=pltpu.SMEM)
    limits = pltpu.CompilerParams(vmem_limit_bytes=8 << 20)

    def in_vmem(*shape):
        return pltpu.VMEM(shape, jnp.float32)

    def in_smem(*shape):
        return pltpu.SMEM(shape, jnp.float32)

    def in_hbm(x):
        return pltpu.with_memory_space_constraint(x, pltpu.HBM)

    def to_vmem(x):
        return pltpu.with_memory_space_constraint(x, pltpu.VMEM)

    def sems(count):
        return pltpu.SemaphoreType.DMA((count,))

    def hold(kernel, name, out_shape, hbm_args, vmem_args, scratch):
        out_space = [smem if x.memory_space == pltpu.SMEM else vmem for x in out_shape]
        return pl.pallas_call(
            kernel,
            out_shape=tuple(out_shape),
            in_specs=[vmem] * len(vmem_args[:-1]) + [hbm] * len(hbm_args) + [vmem] * len(vmem_args[-1:]),
            out_specs=tuple(out_space),
            scratch_shapes=scratch,
            compiler_params=limits,
            cost_estimate=pl.CostEstimate(flops=0, bytes_accessed=4 << 20, transcendentals=0),
            name=name,
        )(*vmem_args[:-1], *(in_hbm(x) for x in hbm_args), *vmem_args[-1:])

    columns_a = blocks // 11 * 6
    rows_a = blocks // 11 * 3

    def factor_part(count):
        return in_vmem(count, kmax, leaf)

    column_other = to_vmem(swap_cores(col_factor))
    row_other = to_vmem(swap_cores(row_factor))

    rates = log_rate
    for axis in range(depth):
        other = swap_owners(rates, bit_of(axis))
        if axis == 0:
            table, near_one, rates, flags, near, part_a = hold(
                first_hold_kernel,
                "hold_first",
                [
                    in_vmem(*per_own),
                    in_vmem(*per_own),
                    in_vmem(*per_own),
                    pltpu.VMEM((depth,) + per_own, jnp.int32),
                    in_vmem(*near_field.shape),
                    factor_part(columns_a),
                ],
                [col_cluster, row_cluster, ranks, near_field, col_factor, rates],
                [],
                [pltpu.VMEM((3, 1, blocks), jnp.int32), in_vmem(*per_own), sems(6)],
            )
            given = jnp.stack([table, near_one])
            given_other = swap_cores(given)
        elif axis == 1:
            part_b, part_c, rates = hold(
                second_hold_kernel,
                "hold_second",
                [factor_part(blocks - columns_a), factor_part(rows_a), in_vmem(*rates.shape)],
                [col_factor, row_factor],
                [given_other, rates],
                [sems(2)],
            )
        elif axis == 2:
            tables, place, part_d, own_a, lift, rates = hold(
                functools.partial(third_hold_kernel, rows_a),
                "hold_third",
                [
                    in_smem(2, *per_own),
                    pltpu.VMEM((2, clusters, blocks), jnp.bfloat16),
                    factor_part(blocks - rows_a),
                    in_vmem(*per_own),
                    in_vmem(*per_own),
                    in_vmem(*rates.shape),
                ],
                [row_factor, log_rate, log_state, load, a_sigma, b_sigma, log_dc],
                [given, given_other, rates],
                [in_vmem(*per_own)] * 5 + [sems(9)],
            )
        shape = (2,) * axis + (1,) * (depth - axis) + per_own
        rates = flat(joined(axis, rates.reshape(shape), other.reshape(shape)))

    known = (place, part_a, part_b, part_c, part_d, column_other, row_other)
    term_scratch = in_vmem(2, blocks, leaf)
    part, rate_one = pl.pallas_call(
        first_kernel,
        out_shape=(in_vmem(clusters, leaf), in_vmem(clusters, leaf)),
        in_specs=[smem] + [vmem] * 9,
        out_specs=(vmem, vmem),
        scratch_shapes=[term_scratch],
        compiler_params=limits,
        name="section_one",
    )(tables, rates, lift, *known)

    all_a = own_a
    for axis in range(depth):
        other = swap_owners(jnp.concatenate([part, all_a], axis=0), bit_of(axis))
        part = part + other[:clusters]
        shape = (2,) * axis + (1,) * (depth - axis) + per_own
        all_a = flat(joined(axis, all_a.reshape(shape), other[clusters:].reshape(shape)))

    part, mid_rate = pl.pallas_call(
        second_kernel,
        out_shape=(in_vmem(clusters, leaf), in_vmem(*per_own)),
        in_specs=[smem] + [vmem] * 10,
        out_specs=(vmem, vmem),
        scratch_shapes=[in_vmem(clusters, leaf), term_scratch],
        compiler_params=limits,
        name="section_two",
    )(tables, part, rate_one, all_a, *known)

    near_two = pl.pallas_call(
        near_kernel,
        out_shape=in_vmem(*per_own),
        in_specs=[vmem, vmem],
        out_specs=vmem,
        scratch_shapes=[in_vmem(*per_own)],
        compiler_params=limits,
        name="near_two",
    )(mid_rate, near)
    near_two = near_two + swap_cores(near_two)

    state_one = jnp.exp(-log_state) - jnp.exp(log_rate - log_dc)
    mid_state = log_state + time_step * state_one
    state_two = jnp.exp(-mid_state) - jnp.exp(mid_rate - log_dc)
    gain_two = 0.5 * time_step / (a_sigma + damping * jnp.exp(mid_rate))
    base_two = 0.5 * (log_rate + mid_rate) + gain_two * (load - b_sigma * state_two)
    new_log_state = log_state + 0.5 * time_step * (state_one + state_two)

    part = part.reshape((2,) * depth + per_own)
    for axis in reversed(range(depth)):
        low = lax.slice_in_dim(part, 0, 1, axis=axis)
        high = lax.slice_in_dim(part, 1, 2, axis=axis)
        send = jnp.where(set_in(axis), low, high)
        keep = jnp.where(set_in(axis), high, low)
        part = keep + swap_owners(flat(send), bit_of(axis)).reshape(keep.shape)
    new_log_rate = base_two - gain_two * (part.reshape(per_own) + near_two)
    return (new_log_rate.reshape(-1), new_log_state.reshape(-1))


def solution(mesh):
    placed = (
        P(("grp", "blk")),
        P(("grp", "blk")),
        P(("grp", "blk")),
        P(("grp", "blk")),
        P(("grp", "blk")),
        P(("grp", "blk")),
        P(("blk", "sub"), None, None),
        P(None, "sub", None),
        P(None, "sub", None),
        P("blk", "sub", None),
        P("blk", "sub", None, None, None),
        P("blk", "sub", None, None, None),
    )
    return jax.shard_map(
        shards,
        mesh=mesh,
        in_specs=placed,
        out_specs=(P(("grp", "blk")), P(("grp", "blk"))),
        check_vma=False,
    )
```

time: 40.8 us -> 40.1 us (0.983)
  waiting for transfers between devices: 12.9 us -> 10.1 us
  Pallas kernels: 6.04 us -> 7.59 us
  starting transfers between devices: 19.9 us -> 20.4 us
    ppermute x2 -> x4, waiting for transfers between devices: 1.94 us -> 0.01 us  [swap_cores(): return lax.ppermute(x, 'sub', [(0, 1), (1, 0)])]
    ppermute x2 -> x4, starting transfers between devices: 0.49 us -> 1.53 us  [swap_cores(): return lax.ppermute(x, 'sub', [(0, 1), (1, 0)])]
    ppermute x9, waiting for transfers between devices: 11 us -> 10.1 us  [swap_owners(): return lax.ppermute(x, ('blk', 'sub'), pairs)]
    pallas_call x1, Pallas kernels: 0.86 us -> 1.45 us  [shards(): pl.pallas_call(second_kernel, out_shape=(in_vmem(clusters, leaf), in_vmem...]
    pallas_call x1, Pallas kernels: 0.85 us -> 1.43 us  [shards(): pl.pallas_call(first_kernel, out_shape=(in_vmem(clusters, leaf), in_vmem(...]
    ppermute x9, starting transfers between devices: 19.4 us -> 18.9 us  [swap_owners(): return lax.ppermute(x, ('blk', 'sub'), pairs)]
    pallas_call x3 -> x4, Pallas kernels: 4.33 us -> 4.71 us  [the longest x3 4.55 us: hold(): pl.pallas_call(kernel, out_shape=tuple(out_shape), in_specs=[vmem] * len(...]
  transfers between devices with their start and end apart: 11 -> 13, of which waited for: 9 -> 7; matrix products, arithmetic and copies ran while one was open for 0% -> 0% of each run, Pallas kernels for 11% -> 12%
where the time goes in v2:
time: 40.1 us; the launch traced here: 39.9 us
  starting transfers between devices  20.4 us (51%)
  waiting for transfers between devices  10.1 us (25%)
  Pallas kernels  7.59 us (19%)
  between operations  0.9 us (2%)
  other arithmetic  0.79 us (2%)
    ppermute x9, starting transfers between devices, swap_owners(): return lax.ppermute(x, ('blk', 'sub'), pairs)  18.9 us
    ppermute x9, waiting for transfers between devices, swap_owners(): return lax.ppermute(x, ('blk', 'sub'), pairs)  10.1 us
    pallas_call x3, Pallas kernels, hold(): pl.pallas_call(kernel, out_shape=tuple(out_shape), in_specs=[vmem] * len(...  4.55 us
    ppermute x4, starting transfers between devices, swap_cores(): return lax.ppermute(x, 'sub', [(0, 1), (1, 0)])  1.53 us
    pallas_call x1, Pallas kernels, shards(): pl.pallas_call(second_kernel, out_shape=(in_vmem(clusters, leaf), in_vmem...  1.45 us
    pallas_call x1, Pallas kernels, shards(): pl.pallas_call(first_kernel, out_shape=(in_vmem(clusters, leaf), in_vmem(...  1.43 us
  transfers between devices with their start and end apart: 13, of which 7 were waited for; matrix products, arithmetic and copies ran while one was open for 0% of the time, Pallas kernels for 12%

profile of v2, /device:TPU:0, one launch (start us, length us, event | category | flops | bytes accessed | tf_op | source)
XLA Modules:
  0.0 39.9 jit_solution(16784980043822993616)
XLA Ops:
  0.6 0.5 %collective-permute-start.4 = (f32[88,48,128]{2,1,0:T(8,128)}, f32[88,48,128]{2,1,0:T(8,128)S(1)}, u32[]{:S(2)}, u32[]{:S(2)}) collective-permute-start(f32[88,48,128]{2,1,0:T(8,128)} %bitcast.135), channel_id=1, source_target_pairs={{0,1},{1,0},{2,3},{3,2},{4,5},{5,4},{6,7},{7,6},{8,9},{9,8},{10,11... | collective-permute-start | bytes 6488072 | tf_op jit(solution)/shard_map/ppermute | solution.py:16
  1.1 0.1 collective-permute-start.5
  1.2 3.7 %collective-permute-start.1 = (f32[8,128]{1,0:T(8,128)}, f32[8,128]{1,0:T(8,128)S(1)}, u32[]{:S(2)}, u32[]{:S(2)}) collective-permute-start(f32[8,128]{1,0:T(8,128)} %bitcast.143), channel_id=1, source_target_pairs={{0,9},{1,8},{2,11},{3,10},{4,13},{5,12},{6,15},{7,14},{8,1},{9,0},... | collective-permute-start | bytes 12296 | tf_op jit(solution)/shard_map/ppermute | solution.py:22
  4.9 1.6 %hold_first.1 = (f32[8,128]{1,0:T(8,128)S(1)}, f32[8,128]{1,0:T(8,128)S(1)}, f32[8,128]{1,0:T(8,128)S(1)}, s32[3,8,128]{2,1,0:T(8,128)S(1)}, f32[4,128,128]{2,1,0:T(8,128)S(1)}, /*index=5*/f32[48,48,128]{2,1,0:T(8,128)S(1)}) custom-call(s32[8,1,88]{2,1,0:T(1,128)} %columns_all.1, s32[8,1,88]{2,1,0:T(1,128)} %rows_all.1, s32[1,1,88]{2,1,0:T(1,128)} %ranks.1, ...), custom_call_target="tpu_custom_call" | custom-call | bytes 4194304 | tf_op jit(solution)/shard_map/hold_first/pallas_call | solution.py:234
  6.6 0.5 %collective-permute-start = (f32[2,8,128]{2,1,0:T(8,128)S(1)}, f32[2,8,128]{2,1,0:T(8,128)S(1)}, u32[]{:S(2)}, u32[]{:S(2)}) collective-permute-start(f32[2,8,128]{2,1,0:T(8,128)S(1)} %pad_maximum_fusion.8.given), channel_id=1, source_target_pairs={{0,1},{1,0},{2,3},{3,2},{4,5},{5,4},{6,7},{7,6},{8,9},{9,8},{10,11... | collective-permute-start | bytes 24584 | tf_op jit(solution)/shard_map/ppermute | solution.py:16
  7.1 0.0 collective-permute-done.1
  7.1 1.3 %collective-permute-start.2 = (f32[16,128]{1,0:T(8,128)S(1)}, f32[16,128]{1,0:T(8,128)S(1)}, u32[]{:S(2)}, u32[]{:S(2)}) collective-permute-start(f32[16,128]{1,0:T(8,128)S(1)} %maximum_bitcast_fusion.own), channel_id=1, source_target_pairs={{0,5},{1,4},{2,7},{3,6},{4,1},{5,0},{6,3},{7,2},{8,13},{9,12},{10,... | collective-permute-start | bytes 24584 | tf_op jit(solution)/shard_map/ppermute | solution.py:22
  8.4 0.0 collective-permute-done.given.given_other
  8.4 1.4 %hold_second.1 = (f32[40,48,128]{2,1,0:T(8,128)S(1)}, f32[24,48,128]{2,1,0:T(8,128)S(1)}, f32[16,128]{1,0:T(8,128)S(1)}) custom-call(f32[2,8,128]{2,1,0:T(8,128)S(1)} %collective-permute-done.given.given_other, f32[88,48,128]{2,1,0:T(8,128)} %bitcast.137, f32[88,48,128]{2,1,0:T(8,128)} %bitcast.139, f32[16,128]{1,0:T(8,128)S(1)} %maximum_bitcast_fusion.own), custom_call_target="tpu_custom_call" | custom-call | bytes 4194304 | tf_op jit(solution)/shard_map/hold_second/pallas_call | solution.py:234
  9.8 0.4 %collective-permute-done.2 = f32[16,128]{1,0:T(8,128)S(1)} collective-permute-done((f32[16,128]{1,0:T(8,128)S(1)}, f32[16,128]{1,0:T(8,128)S(1)}, u32[]{:S(2)}, u32[]{:S(2)}) %collective-permute-start.2) | collective-permute-done | bytes 8224 | tf_op jit(solution)/shard_map/ppermute | solution.py:22
  10.3 2.0 %collective-permute-start.3 = (f32[32,128]{1,0:T(8,128)S(1)}, f32[32,128]{1,0:T(8,128)S(1)}, u32[]{:S(2)}, u32[]{:S(2)}) collective-permute-start(f32[32,128]{1,0:T(8,128)S(1)} %bitcast.129), channel_id=1, source_target_pairs={{0,3},{1,2},{2,1},{3,0},{4,7},{5,6},{6,5},{7,4},{8,11},{9,10},{10,... | collective-permute-start | bytes 49160 | tf_op jit(solution)/shard_map/ppermute | solution.py:22
  12.2 1.5 %hold_third.1 = (f32[2,8,128]{2,1,0:T(8,128)S(4)}, bf16[2,64,88]{2,1,0:T(8,128)(2,1)S(1)}, f32[64,48,128]{2,1,0:T(8,128)S(1)}, f32[8,128]{1,0:T(8,128)S(1)}, f32...) custom-call(f32[2,8,128]{2,1,0:T(8,128)S(1)} %pad_maximum_fusion.8.given, ...), custom_call_target="tpu_custom_call" | custom-call | bytes 4194304 | tf_op jit(solution)/shard_map/hold_third/pallas_call | solution.py:234
  13.8 0.0 collective-permute-done.3
  13.8 0.0 collective-permute-done.4.refs_5_
  13.8 0.0 collective-permute-done.5.refs_6_
  13.8 1.4 %section_one.1 = (f32[64,128]{1,0:T(8,128)S(1)}, f32[64,128]{1,0:T(8,128)S(1)}) custom-call(f32[2,8,128]{2,1,0:T(8,128)S(4)} %get-tuple-element.26.tables, f32[64,128]{1,0:T(8,128)S(1)} %bitcast.128, f32[8,128]{1,0:T(8,128)S(1)} %get-tuple-element.28.lift, bf16[2,64,88]{2,1,0:T(8,128)(2,1)S(1)} %get-tuple-element.29.refs_0_, ...), custom_call_target="tpu_custom_call" | custom-call | tf_op jit(solution)/shard_map/section_one/pallas_call | solution.py:305
  15.3 1.8 %collective-permute-start.6 = (f32[72,128]{1,0:T(8,128)S(1)}, f32[72,128]{1,0:T(8,128)S(1)}, u32[]{:S(2)}, u32[]{:S(2)}) collective-permute-start(f32[72,128]{1,0:T(8,128)S(1)} %pad_maximum_fusion.2), channel_id=1, source_target_pairs={{0,9},{1,8},{2,11},{3,10},{4,13},{5,12},{6,15},{7,14},{8,1},{9,0},... | collective-permute-start | bytes 110600 | tf_op jit(solution)/shard_map/ppermute | solution.py:22
  17.1 2.6 %collective-permute-done.6 = f32[72,128]{1,0:T(8,128)S(1)} collective-permute-done((f32[72,128]{1,0:T(8,128)S(1)}, f32[72,128]{1,0:T(8,128)S(1)}, u32[]{:S(2)}, u32[]{:S(2)}) %collective-permute-start.6) | collective-permute-done | bytes 36896 | tf_op jit(solution)/shard_map/ppermute | solution.py:22
  19.7 1.8 %collective-permute-start.7 = (f32[80,128]{1,0:T(8,128)S(1)}, f32[80,128]{1,0:T(8,128)S(1)}, u32[]{:S(2)}, u32[]{:S(2)}) collective-permute-start(f32[80,128]{1,0:T(8,128)S(1)} %pad_maximum_fusion.1), channel_id=1, source_target_pairs={{0,5},{1,4},{2,7},{3,6},{4,1},{5,0},{6,3},{7,2},{8,13},{9,12},{10,... | collective-permute-start | bytes 122888 | tf_op jit(solution)/shard_map/ppermute | solution.py:22
  21.5 1.7 %collective-permute-done.7 = f32[80,128]{1,0:T(8,128)S(1)} collective-permute-done((f32[80,128]{1,0:T(8,128)S(1)}, f32[80,128]{1,0:T(8,128)S(1)}, u32[]{:S(2)}, u32[]{:S(2)}) %collective-permute-start.7) | collective-permute-done | bytes 40992 | tf_op jit(solution)/shard_map/ppermute | solution.py:22
  23.2 1.8 %collective-permute-start.8 = (f32[96,128]{1,0:T(8,128)S(1)}, f32[96,128]{1,0:T(8,128)S(1)}, u32[]{:S(2)}, u32[]{:S(2)}) collective-permute-start(f32[96,128]{1,0:T(8,128)S(1)} %pad_maximum_fusion), channel_id=1, source_target_pairs={{0,3},{1,2},{2,1},{3,0},{4,7},{5,6},{6,5},{7,4},{8,11},{9,10},{10,... | collective-permute-start | bytes 147464 | tf_op jit(solution)/shard_map/ppermute | solution.py:22
  25.1 1.8 %collective-permute-done.8 = f32[96,128]{1,0:T(8,128)S(1)} collective-permute-done((f32[96,128]{1,0:T(8,128)S(1)}, f32[96,128]{1,0:T(8,128)S(1)}, u32[]{:S(2)}, u32[]{:S(2)}) %collective-permute-start.8) | collective-permute-done | bytes 49184 | tf_op jit(solution)/shard_map/ppermute | solution.py:22
  26.9 0.0 copy-start
  27.0 0.0 copy-start.1
  27.0 0.0 copy-start.2
  27.0 0.0 copy-start.3
  27.0 0.0 copy-start.4
  27.0 0.0 copy-start.5
  27.0 1.4 %section_two.1 = (f32[64,128]{1,0:T(8,128)S(1)}, f32[8,128]{1,0:T(8,128)S(1)}) custom-call(f32[2,8,128]{2,1,0:T(8,128)S(4)} %get-tuple-element.26.tables, f32[64,128]{1,0:T(8,128)S(1)} %slice_add_fusion.lifted, f32[64,128]{1,0:T(8,128)S(1)} %get-tuple-element.36.rate_one, f32[64,128]{1,0:T(8,128)S(1)} %bitcast.127, ...), custom_call_target="tpu_custom_call" | custom-call | tf_op jit(solution)/shard_map/section_two/pallas_call | solution.py:322
  28.5 2.0 %collective-permute-start.9 = (f32[32,128]{1,0:T(8,128)S(1)}, f32[32,128]{1,0:T(8,128)S(1)}, u32[]{:S(2)}, u32[]{:S(2)}) collective-permute-start(f32[32,128]{1,0:T(8,128)S(1)} %bitcast.151), channel_id=1, source_target_pairs={{0,3},{1,2},{2,1},{3,0},{4,7},{5,6},{6,5},{7,4},{8,11},{9,10},{10,... | collective-permute-start | bytes 49160 | tf_op jit(solution)/shard_map/ppermute | solution.py:22
  30.5 1.4 %collective-permute-done.9 = f32[32,128]{1,0:T(8,128)S(1)} collective-permute-done((f32[32,128]{1,0:T(8,128)S(1)}, f32[32,128]{1,0:T(8,128)S(1)}, u32[]{:S(2)}, u32[]{:S(2)}) %collective-permute-start.9) | collective-permute-done | bytes 16416 | tf_op jit(solution)/shard_map/ppermute | solution.py:22
  31.9 1.9 %collective-permute-start.10 = (f32[16,128]{1,0:T(8,128)S(1)}, f32[16,128]{1,0:T(8,128)S(1)}, u32[]{:S(2)}, u32[]{:S(2)}) collective-permute-start(f32[16,128]{1,0:T(8,128)S(1)} %select_bitcast_fusion), channel_id=1, source_target_pairs={{0,5},{1,4},{2,7},{3,6},{4,1},{5,0},{6,3},{7,2},{8,13},{9,12},{10,... | collective-permute-start | bytes 24584 | tf_op jit(solution)/shard_map/ppermute | solution.py:22
  33.8 0.2 near_two.1
  34.0 0.4 %collective-permute-start.12 = (f32[8,128]{1,0:T(8,128)S(1)}, f32[8,128]{1,0:T(8,128)S(1)}, u32[]{:S(2)}, u32[]{:S(2)}) collective-permute-start(f32[8,128]{1,0:T(8,128)S(1)} %near_two.1), channel_id=1, source_target_pairs={{0,1},{1,0},{2,3},{3,2},{4,5},{5,4},{6,7},{7,6},{8,9},{9,8},{10,11... | collective-permute-start | bytes 12296 | tf_op jit(solution)/shard_map/ppermute | solution.py:16
  34.4 0.8 %collective-permute-done.10 = f32[16,128]{1,0:T(8,128)S(1)} collective-permute-done((f32[16,128]{1,0:T(8,128)S(1)}, f32[16,128]{1,0:T(8,128)S(1)}, u32[]{:S(2)}, u32[]{:S(2)}) %collective-permute-start.10) | collective-permute-done | bytes 8224 | tf_op jit(solution)/shard_map/ppermute | solution.py:22
  35.2 2.6 %collective-permute-start.11 = (f32[8,128]{1,0:T(8,128)S(1)}, f32[8,128]{1,0:T(8,128)S(1)}, u32[]{:S(2)}, u32[]{:S(2)}) collective-permute-start(f32[8,128]{1,0:T(8,128)S(1)} %fusion.6), channel_id=1, source_target_pairs={{0,9},{1,8},{2,11},{3,10},{4,13},{5,12},{6,15},{7,14},{8,1},{9,0},... | collective-permute-start | bytes 12296 | tf_op jit(solution)/shard_map/ppermute | solution.py:22
  37.8 0.0 collective-permute-done.12
  37.9 1.4 %collective-permute-done.11 = f32[8,128]{1,0:T(8,128)S(1)} collective-permute-done((f32[8,128]{1,0:T(8,128)S(1)}, f32[8,128]{1,0:T(8,128)S(1)}, u32[]{:S(2)}, u32[]{:S(2)}) %collective-permute-start.11) | collective-permute-done | bytes 4128 | tf_op jit(solution)/shard_map/ppermute | solution.py:22
  39.2 0.0 copy-done
  39.2 0.0 copy-done.1
  39.2 0.0 copy-done.2
  39.2 0.0 copy-done.3
  39.2 0.0 copy-done.4
  39.2 0.0 copy-done.5
  39.3 0.6 %add_bitcast_fusion = (f32[1024]{0:T(1024)}, f32[1024]{0:T(1024)}) fusion(f32[8,128]{1,0:T(8,128)S(1)} %get-tuple-element.37.mid_rate, f32[1024]{0:T(1024)S(1)} %copy-done.5, f32[1024]{0:T(1024)S(1)} %copy-done.1, f32[1024]{0:T(1024)S(1)} %copy-done, f32[8,128]{1,0:T(8,128)S(1)} %near_two.1, f32[8,128]{1,0:T(8,128)S(1)} %collective-permute-done.12, ...), kind=kLoop, calls=%fused_computation.40 | loop fusion | flops 26624 | bytes 58368 | tf_op jit(solution)/shard_map/reshape | solution.py:358
  (36 shorter events, 0.2 us)
Async XLA Ops:
  0.6 13.2 %collective-permute-start.4 = (f32[88,48,128]{2,1,0:T(8,128)}, f32[88,48,128]{2,1,0:T(8,128)S(1)}, u32[]{:S(2)}, u32[]{:S(2)}) collective-permute-start(f32[88,48,128]{2,1,0:T(8,128)} %bitcast.135), channel_id=1, source_target_pairs={{0,1},{1,0},{2,3},{3,2},{4,5},{5,4},{6,7},{7,6},{8,9},{9,8},{10,11... | collective-permute-start | bytes 6488072 | tf_op jit(solution)/shard_map/ppermute | solution.py:16
  1.1 12.7 %collective-permute-start.5 = (f32[88,48,128]{2,1,0:T(8,128)}, f32[88,48,128]{2,1,0:T(8,128)S(1)}, u32[]{:S(2)}, u32[]{:S(2)}) collective-permute-start(f32[88,48,128]{2,1,0:T(8,128)} %bitcast.138), channel_id=1, source_target_pairs={{0,1},{1,0},{2,3},{3,2},{4,5},{5,4},{6,7},{7,6},{8,9},{9,8},{10,11... | collective-permute-start | bytes 6488072 | tf_op jit(solution)/shard_map/ppermute | solution.py:16
  1.2 5.9 %collective-permute-start.1 = (f32[8,128]{1,0:T(8,128)}, f32[8,128]{1,0:T(8,128)S(1)}, u32[]{:S(2)}, u32[]{:S(2)}) collective-permute-start(f32[8,128]{1,0:T(8,128)} %bitcast.143), channel_id=1, source_target_pairs={{0,9},{1,8},{2,11},{3,10},{4,13},{5,12},{6,15},{7,14},{8,1},{9,0},... | collective-permute-start | bytes 12296 | tf_op jit(solution)/shard_map/ppermute | solution.py:22
  6.6 1.9 %collective-permute-start = (f32[2,8,128]{2,1,0:T(8,128)S(1)}, f32[2,8,128]{2,1,0:T(8,128)S(1)}, u32[]{:S(2)}, u32[]{:S(2)}) collective-permute-start(f32[2,8,128]{2,1,0:T(8,128)S(1)} %pad_maximum_fusion.8.given), channel_id=1, source_target_pairs={{0,1},{1,0},{2,3},{3,2},{4,5},{5,4},{6,7},{7,6},{8,9},{9,8},{10,11... | collective-permute-start | bytes 24584 | tf_op jit(solution)/shard_map/ppermute | solution.py:16
  7.1 3.1 %collective-permute-start.2 = (f32[16,128]{1,0:T(8,128)S(1)}, f32[16,128]{1,0:T(8,128)S(1)}, u32[]{:S(2)}, u32[]{:S(2)}) collective-permute-start(f32[16,128]{1,0:T(8,128)S(1)} %maximum_bitcast_fusion.own), channel_id=1, source_target_pairs={{0,5},{1,4},{2,7},{3,6},{4,1},{5,0},{6,3},{7,2},{8,13},{9,12},{10,... | collective-permute-start | bytes 24584 | tf_op jit(solution)/shard_map/ppermute | solution.py:22
  10.3 3.5 %collective-permute-start.3 = (f32[32,128]{1,0:T(8,128)S(1)}, f32[32,128]{1,0:T(8,128)S(1)}, u32[]{:S(2)}, u32[]{:S(2)}) collective-permute-start(f32[32,128]{1,0:T(8,128)S(1)} %bitcast.129), channel_id=1, source_target_pairs={{0,3},{1,2},{2,1},{3,0},{4,7},{5,6},{6,5},{7,4},{8,11},{9,10},{10,... | collective-permute-start | bytes 49160 | tf_op jit(solution)/shard_map/ppermute | solution.py:22
  15.3 4.4 %collective-permute-start.6 = (f32[72,128]{1,0:T(8,128)S(1)}, f32[72,128]{1,0:T(8,128)S(1)}, u32[]{:S(2)}, u32[]{:S(2)}) collective-permute-start(f32[72,128]{1,0:T(8,128)S(1)} %pad_maximum_fusion.2), channel_id=1, source_target_pairs={{0,9},{1,8},{2,11},{3,10},{4,13},{5,12},{6,15},{7,14},{8,1},{9,0},... | collective-permute-start | bytes 110600 | tf_op jit(solution)/shard_map/ppermute | solution.py:22
  19.7 3.5 %collective-permute-start.7 = (f32[80,128]{1,0:T(8,128)S(1)}, f32[80,128]{1,0:T(8,128)S(1)}, u32[]{:S(2)}, u32[]{:S(2)}) collective-permute-start(f32[80,128]{1,0:T(8,128)S(1)} %pad_maximum_fusion.1), channel_id=1, source_target_pairs={{0,5},{1,4},{2,7},{3,6},{4,1},{5,0},{6,3},{7,2},{8,13},{9,12},{10,... | collective-permute-start | bytes 122888 | tf_op jit(solution)/shard_map/ppermute | solution.py:22
  23.2 3.6 %collective-permute-start.8 = (f32[96,128]{1,0:T(8,128)S(1)}, f32[96,128]{1,0:T(8,128)S(1)}, u32[]{:S(2)}, u32[]{:S(2)}) collective-permute-start(f32[96,128]{1,0:T(8,128)S(1)} %pad_maximum_fusion), channel_id=1, source_target_pairs={{0,3},{1,2},{2,1},{3,0},{4,7},{5,6},{6,5},{7,4},{8,11},{9,10},{10,... | collective-permute-start | bytes 147464 | tf_op jit(solution)/shard_map/ppermute | solution.py:22
  26.9 12.3 %copy-start = (f32[1024]{0:T(1024)S(1)}, f32[1024]{0:T(1024)}, u32[]{:S(2)}) copy-start(f32[1024]{0:T(1024)} %param.12) | copy-start | bytes 12292
  27.0 12.3 %copy-start.1 = (f32[1024]{0:T(1024)S(1)}, f32[1024]{0:T(1024)}, u32[]{:S(2)}) copy-start(f32[1024]{0:T(1024)} %param.13) | copy-start | bytes 12292
  27.0 12.3 %copy-start.2 = (f32[1024]{0:T(1024)S(1)}, f32[1024]{0:T(1024)}, u32[]{:S(2)}) copy-start(f32[1024]{0:T(1024)} %param.14) | copy-start | bytes 12292
  27.0 12.2 %copy-start.3 = (f32[1024]{0:T(1024)S(1)}, f32[1024]{0:T(1024)}, u32[]{:S(2)}) copy-start(f32[1024]{0:T(1024)} %param.15) | copy-start | bytes 12292
  27.0 12.2 %copy-start.4 = (f32[1024]{0:T(1024)S(1)}, f32[1024]{0:T(1024)}, u32[]{:S(2)}) copy-start(f32[1024]{0:T(1024)} %param.16) | copy-start | bytes 12292
  27.0 12.2 %copy-start.5 = (f32[1024]{0:T(1024)S(1)}, f32[1024]{0:T(1024)}, u32[]{:S(2)}) copy-start(f32[1024]{0:T(1024)} %param.17) | copy-start | bytes 12292
  28.5 3.4 %collective-permute-start.9 = (f32[32,128]{1,0:T(8,128)S(1)}, f32[32,128]{1,0:T(8,128)S(1)}, u32[]{:S(2)}, u32[]{:S(2)}) collective-permute-start(f32[32,128]{1,0:T(8,128)S(1)} %bitcast.151), channel_id=1, source_target_pairs={{0,3},{1,2},{2,1},{3,0},{4,7},{5,6},{6,5},{7,4},{8,11},{9,10},{10,... | collective-permute-start | bytes 49160 | tf_op jit(solution)/shard_map/ppermute | solution.py:22
  31.9 3.2 %collective-permute-start.10 = (f32[16,128]{1,0:T(8,128)S(1)}, f32[16,128]{1,0:T(8,128)S(1)}, u32[]{:S(2)}, u32[]{:S(2)}) collective-permute-start(f32[16,128]{1,0:T(8,128)S(1)} %select_bitcast_fusion), channel_id=1, source_target_pairs={{0,5},{1,4},{2,7},{3,6},{4,1},{5,0},{6,3},{7,2},{8,13},{9,12},{10,... | collective-permute-start | bytes 24584 | tf_op jit(solution)/shard_map/ppermute | solution.py:22
  34.0 3.9 %collective-permute-start.12 = (f32[8,128]{1,0:T(8,128)S(1)}, f32[8,128]{1,0:T(8,128)S(1)}, u32[]{:S(2)}, u32[]{:S(2)}) collective-permute-start(f32[8,128]{1,0:T(8,128)S(1)} %near_two.1), channel_id=1, source_target_pairs={{0,1},{1,0},{2,3},{3,2},{4,5},{5,4},{6,7},{7,6},{8,9},{9,8},{10,11... | collective-permute-start | bytes 12296 | tf_op jit(solution)/shard_map/ppermute | solution.py:16
  35.2 4.0 %collective-permute-start.11 = (f32[8,128]{1,0:T(8,128)S(1)}, f32[8,128]{1,0:T(8,128)S(1)}, u32[]{:S(2)}, u32[]{:S(2)}) collective-permute-start(f32[8,128]{1,0:T(8,128)S(1)} %fusion.6), channel_id=1, source_target_pairs={{0,9},{1,8},{2,11},{3,10},{4,13},{5,12},{6,15},{7,14},{8,1},{9,0},... | collective-permute-start | bytes 12296 | tf_op jit(solution)/shard_map/ppermute | solution.py:22

commit v3 on v2

--- a/solution.py
+++ b/solution.py
@@ -16,9 +16,12 @@
     return lax.ppermute(x, "sub", [(0, 1), (1, 0)])
 
 
-def swap_owners(x, bit):
+def swap_owners(x, bit, odd_bit=None):
     owners = lax.axis_size("blk")
-    pairs = [(2 * c + s, 2 * (c ^ bit) + 1 - s) for c in range(owners) for s in range(2)]
+    bits = (bit, bit if odd_bit is None else odd_bit)
+    pairs = [
+        (2 * c + s, 2 * (c ^ bits[(c.bit_count() + s) % 2]) + 1 - s) for c in range(owners) for s in range(2)
+    ]
     return lax.ppermute(x, ("blk", "sub"), pairs)
 
 
@@ -70,11 +73,15 @@
     table[...] = jnp.zeros(table.shape, jnp.float32)
     for i in range(3):
         table[pl.ds(i, 1), pl.ds(0, numbers.shape[2])] = numbers[i].astype(jnp.float32)
-    bit = lax.broadcasted_iota(jnp.int32, flags.shape, 0)
-    flags[...] = lax.shift_right_logical(device, bit) & 1
-
-
-def second_hold_kernel(given, columns, rows, own, held_columns, held_rows, own_copy, sems):
+    parity = lax.axis_index("sub")
+    for i in range(flags.shape[0] - 1):
+        bit = lax.shift_right_logical(device, i) & 1
+        parity = parity + bit
+        flags[i] = jnp.full(flags.shape[1:], bit, jnp.int32)
+    flags[flags.shape[0] - 1] = jnp.full(flags.shape[1:], parity & 1, jnp.int32)
+
+
+def second_hold_kernel(columns, rows, own, held_columns, held_rows, own_copy, sems):
     done = columns.shape[0] - held_columns.shape[0]
     run_copies(pieces_of(columns, held_columns, done) + pieces_of(rows, held_rows), sems)
     own_copy[...] = own[...]
@@ -202,9 +209,23 @@
     def set_in(axis):
         return flags[depth - 1 - axis] != 0
 
-    def joined(axis, own, other):
-        first, second = jnp.where(set_in(axis), other, own), jnp.where(set_in(axis), own, other)
-        return jnp.concatenate([first, second], axis=axis)
+    def joined(flag, axis, own, other):
+        return jnp.concatenate([jnp.where(flag, other, own), jnp.where(flag, own, other)], axis=axis)
+
+    even_axes = list(range(depth))
+    odd_axes = even_axes[::-1]
+
+    def by_kind(even, odd):
+        return jnp.where(flags[depth] != 0, odd, even)
+
+    def set_at(step):
+        return by_kind(flags[depth - 1 - even_axes[step]], flags[depth - 1 - odd_axes[step]]) != 0
+
+    def hop(x, step):
+        return swap_owners(x, bit_of(even_axes[step]), bit_of(odd_axes[step]))
+
+    def rest(axes):
+        return list(axes) + [depth, depth + 1]
 
     def flat(x):
         return x.reshape(-1, leaf)
@@ -242,7 +263,7 @@
             name=name,
         )(*vmem_args[:-1], *(in_hbm(x) for x in hbm_args), *vmem_args[-1:])
 
-    columns_a = blocks // 11 * 6
+    columns_a = blocks // 11 * 4
     rows_a = blocks // 11 * 3
 
     def factor_part(count):
@@ -262,7 +283,7 @@
                     in_vmem(*per_own),
                     in_vmem(*per_own),
                     in_vmem(*per_own),
-                    pltpu.VMEM((depth,) + per_own, jnp.int32),
+                    pltpu.VMEM((depth + 1,) + per_own, jnp.int32),
                     in_vmem(*near_field.shape),
                     factor_part(columns_a),
                 ],
@@ -270,7 +291,7 @@
                 [],
                 [pltpu.VMEM((3, 1, blocks), jnp.int32), in_vmem(*per_own), sems(6)],
             )
-            given = jnp.stack([table, near_one])
+            given = jnp.concatenate([jnp.stack([table, near_one]), flags.astype(jnp.float32)], axis=0)
             given_other = swap_cores(given)
         elif axis == 1:
             part_b, part_c, rates = hold(
@@ -278,7 +299,7 @@
                 "hold_second",
                 [factor_part(blocks - columns_a), factor_part(rows_a), in_vmem(*rates.shape)],
                 [col_factor, row_factor],
-                [given_other, rates],
+                [rates],
                 [sems(2)],
             )
         elif axis == 2:
@@ -298,7 +319,8 @@
                 [in_vmem(*per_own)] * 5 + [sems(9)],
             )
         shape = (2,) * axis + (1,) * (depth - axis) + per_own
-        rates = flat(joined(axis, rates.reshape(shape), other.reshape(shape)))
+        flag = given_other[2 + depth - 1 - axis] != 0 if axis == 1 else set_in(axis)
+        rates = flat(joined(flag, axis, rates.reshape(shape), other.reshape(shape)))
 
     known = (place, part_a, part_b, part_c, part_d, column_other, row_other)
     term_scratch = in_vmem(2, blocks, leaf)
@@ -312,12 +334,19 @@
         name="section_one",
     )(tables, rates, lift, *known)
 
-    all_a = own_a
-    for axis in range(depth):
-        other = swap_owners(jnp.concatenate([part, all_a], axis=0), bit_of(axis))
+    all_a = own_a[None]
+    for step in range(depth):
+        other = hop(jnp.concatenate([part, flat(all_a)], axis=0), step)
         part = part + other[:clusters]
-        shape = (2,) * axis + (1,) * (depth - axis) + per_own
-        all_a = flat(joined(axis, all_a.reshape(shape), other[clusters:].reshape(shape)))
+        all_a = joined(set_at(step), 0, all_a, other[clusters:].reshape(all_a.shape))
+    all_a = all_a.reshape((2,) * depth + per_own)
+    all_a = by_kind(
+        *(
+            jnp.transpose(all_a, rest(axes[::-1].index(axis) for axis in range(depth)))
+            for axes in (even_axes, odd_axes)
+        )
+    )
+    all_a = flat(all_a)
 
     part, mid_rate = pl.pallas_call(
         second_kernel,
@@ -348,7 +377,7 @@
     new_log_state = log_state + 0.5 * time_step * (state_one + state_two)
 
     part = part.reshape((2,) * depth + per_own)
-    for axis in reversed(range(depth)):
+    for axis in range(depth):
         low = lax.slice_in_dim(part, 0, 1, axis=axis)
         high = lax.slice_in_dim(part, 1, 2, axis=axis)
         send = jnp.where(set_in(axis), low, high)

time: 40.1 us -> 39.2 us (0.978)
  starting transfers between devices: 20.4 us -> 18 us
  waiting for transfers between devices: 10.1 us -> 11.6 us
    ppermute x9, starting transfers between devices: 18.9 us -> 16.7 us  [swap_owners(): return lax.ppermute(x, ('blk', 'sub'), pairs)]
    ppermute x9, waiting for transfers between devices: 10.1 us -> 11.6 us  [swap_owners(): return lax.ppermute(x, ('blk', 'sub'), pairs)]
  transfers between devices with their start and end apart: 13 -> 13, of which waited for: 7 -> 8; matrix products, arithmetic and copies ran while one was open for 0% -> 0% of each run, Pallas kernels for 12% -> 12%
where the time goes in v3:
time: 39.2 us; the launch traced here: 39 us
  starting transfers between devices  18 us (46%)
  waiting for transfers between devices  11.6 us (30%)
  Pallas kernels  7.6 us (19%)
  between operations  0.86 us (2%)
  other arithmetic  0.83 us (2%)
    ppermute x9, starting transfers between devices, swap_owners(): return lax.ppermute(x, ('blk', 'sub'), pairs)  16.7 us
    ppermute x9, waiting for transfers between devices, swap_owners(): return lax.ppermute(x, ('blk', 'sub'), pairs)  11.6 us
    pallas_call x3, Pallas kernels, hold(): pl.pallas_call(kernel, out_shape=tuple(out_shape), in_specs=[vmem] * len(...  4.53 us
    pallas_call x1, Pallas kernels, shards(): pl.pallas_call(second_kernel, out_shape=(in_vmem(clusters, leaf), in_vmem...  1.46 us
    pallas_call x1, Pallas kernels, shards(): pl.pallas_call(first_kernel, out_shape=(in_vmem(clusters, leaf), in_vmem(...  1.45 us
    ppermute x4, starting transfers between devices, swap_cores(): return lax.ppermute(x, 'sub', [(0, 1), (1, 0)])  1.37 us
  transfers between devices with their start and end apart: 13, of which 8 were waited for; matrix products, arithmetic and copies ran while one was open for 0% of the time, Pallas kernels for 12%

profile of v3, /device:TPU:0, one launch (start us, length us, event | category | flops | bytes accessed | tf_op | source)
XLA Modules:
  0.0 39.0 jit_solution(6176611322177809691)
XLA Ops:
  0.6 0.5 %collective-permute-start.4 = (f32[88,48,128]{2,1,0:T(8,128)}, f32[88,48,128]{2,1,0:T(8,128)S(1)}, u32[]{:S(2)}, u32[]{:S(2)}) collective-permute-start(f32[88,48,128]{2,1,0:T(8,128)} %bitcast.126), channel_id=1, source_target_pairs={{0,1},{1,0},{2,3},{3,2},{4,5},{5,4},{6,7},{7,6},{8,9},{9,8},{10,11... | collective-permute-start | bytes 6488072 | tf_op jit(solution)/shard_map/ppermute | solution.py:16
  1.1 0.1 collective-permute-start.5
  1.2 3.7 %collective-permute-start.1 = (f32[8,128]{1,0:T(8,128)}, f32[8,128]{1,0:T(8,128)S(1)}, u32[]{:S(2)}, u32[]{:S(2)}) collective-permute-start(f32[8,128]{1,0:T(8,128)} %bitcast.135), channel_id=1, source_target_pairs={{0,9},{1,8},{2,11},{3,10},{4,13},{5,12},{6,15},{7,14},{8,1},{9,0},... | collective-permute-start | bytes 12296 | tf_op jit(solution)/shard_map/ppermute | solution.py:25
  4.9 1.5 %hold_first.1 = (f32[8,128]{1,0:T(8,128)S(1)}, f32[8,128]{1,0:T(8,128)S(1)}, f32[8,128]{1,0:T(8,128)S(1)}, s32[4,8,128]{2,1,0:T(8,128)S(1)}, f32[4,128,128]{2,1,0:T(8,128)S(1)}, /*index=5*/f32[32,48,128]{2,1,0:T(8,128)S(1)}) custom-call(s32[8,1,88]{2,1,0:T(1,128)} %columns_all.1, s32[8,1,88]{2,1,0:T(1,128)} %rows_all.1, s32[1,1,88]{2,1,0:T(1,128)} %ranks.1, ...), custom_call_target="tpu_custom_call" | custom-call | bytes 4194304 | tf_op jit(solution)/shard_map/hold_first/pallas_call | solution.py:255
  6.5 0.5 %collective-permute-start = (f32[6,8,128]{2,1,0:T(8,128)S(1)}, f32[6,8,128]{2,1,0:T(8,128)S(1)}, u32[]{:S(2)}, u32[]{:S(2)}) collective-permute-start(f32[6,8,128]{2,1,0:T(8,128)S(1)} %pad_maximum_fusion.5.given), channel_id=1, source_target_pairs={{0,1},{1,0},{2,3},{3,2},{4,5},{5,4},{6,7},{7,6},{8,9},{9,8},{10,11... | collective-permute-start | bytes 73736 | tf_op jit(solution)/shard_map/ppermute | solution.py:16
  7.0 0.0 collective-permute-done.1
  7.0 1.3 %collective-permute-start.2 = (f32[16,128]{1,0:T(8,128)S(1)}, f32[16,128]{1,0:T(8,128)S(1)}, u32[]{:S(2)}, u32[]{:S(2)}) collective-permute-start(f32[16,128]{1,0:T(8,128)S(1)} %maximum_bitcast_fusion.own), channel_id=1, source_target_pairs={{0,5},{1,4},{2,7},{3,6},{4,1},{5,0},{6,3},{7,2},{8,13},{9,12},{10,... | collective-permute-start | bytes 24584 | tf_op jit(solution)/shard_map/ppermute | solution.py:25
  8.3 1.5 %hold_second.1 = (f32[56,48,128]{2,1,0:T(8,128)S(1)}, f32[24,48,128]{2,1,0:T(8,128)S(1)}, f32[16,128]{1,0:T(8,128)S(1)}) custom-call(f32[88,48,128]{2,1,0:T(8,128)} %bitcast.128, f32[88,48,128]{2,1,0:T(8,128)} %bitcast.130, f32[16,128]{1,0:T(8,128)S(1)} %maximum_bitcast_fusion.own), custom_call_target="tpu_custom_call" | custom-call | bytes 4194304 | tf_op jit(solution)/shard_map/hold_second/pallas_call | solution.py:255
  9.8 0.0 collective-permute-done.given_other
  9.8 0.3 collective-permute-done.2
  10.1 1.3 %collective-permute-start.3 = (f32[32,128]{1,0:T(8,128)S(1)}, f32[32,128]{1,0:T(8,128)S(1)}, u32[]{:S(2)}, u32[]{:S(2)}) collective-permute-start(f32[32,128]{1,0:T(8,128)S(1)} %bitcast.121), channel_id=1, source_target_pairs={{0,3},{1,2},{2,1},{3,0},{4,7},{5,6},{6,5},{7,4},{8,11},{9,10},{10,... | collective-permute-start | bytes 49160 | tf_op jit(solution)/shard_map/ppermute | solution.py:25
  11.5 1.5 %hold_third.1 = (f32[2,8,128]{2,1,0:T(8,128)S(4)}, bf16[2,64,88]{2,1,0:T(8,128)(2,1)S(1)}, f32[64,48,128]{2,1,0:T(8,128)S(1)}, f32[8,128]{1,0:T(8,128)S(1)}, f32...) custom-call(f32[6,8,128]{2,1,0:T(8,128)S(1)} %pad_maximum_fusion.5.given, f32[6,8,128]{2,1,0:T(8,128)S(1)} %collective-permute-done.given_other, ...), custom_call_target="tpu_custom_call" | custom-call | bytes 4194304 | tf_op jit(solution)/shard_map/hold_third/pallas_call | solution.py:255
  13.0 0.3 collective-permute-done.3
  13.4 0.0 collective-permute-done.4.refs_5_
  13.4 0.0 collective-permute-done.5.refs_6_
  13.4 1.4 %section_one.1 = (f32[64,128]{1,0:T(8,128)S(1)}, f32[64,128]{1,0:T(8,128)S(1)}) custom-call(f32[2,8,128]{2,1,0:T(8,128)S(4)} %get-tuple-element.26.tables, f32[64,128]{1,0:T(8,128)S(1)} %bitcast.120, f32[8,128]{1,0:T(8,128)S(1)} %get-tuple-element.28.lift, bf16[2,64,88]{2,1,0:T(8,128)(2,1)S(1)} %get-tuple-element.29.refs_0_, ...), custom_call_target="tpu_custom_call" | custom-call | tf_op jit(solution)/shard_map/section_one/pallas_call | solution.py:327
  14.9 2.3 %collective-permute-start.6 = (f32[72,128]{1,0:T(8,128)S(1)}, f32[72,128]{1,0:T(8,128)S(1)}, u32[]{:S(2)}, u32[]{:S(2)}) collective-permute-start(f32[72,128]{1,0:T(8,128)S(1)} %pad_maximum_fusion.2), channel_id=1, source_target_pairs={{0,9},{1,2},{2,1},{3,10},{4,7},{5,12},{6,15},{7,4},{8,11},{9,0},{1... | collective-permute-start | bytes 110600 | tf_op jit(solution)/shard_map/ppermute | solution.py:25
  17.1 2.1 %collective-permute-done.6 = f32[72,128]{1,0:T(8,128)S(1)} collective-permute-done((f32[72,128]{1,0:T(8,128)S(1)}, f32[72,128]{1,0:T(8,128)S(1)}, u32[]{:S(2)}, u32[]{:S(2)}) %collective-permute-start.6) | collective-permute-done | bytes 36896 | tf_op jit(solution)/shard_map/ppermute | solution.py:25
  19.3 1.4 %collective-permute-start.7 = (f32[80,128]{1,0:T(8,128)S(1)}, f32[80,128]{1,0:T(8,128)S(1)}, u32[]{:S(2)}, u32[]{:S(2)}) collective-permute-start(f32[80,128]{1,0:T(8,128)S(1)} %pad_maximum_fusion.1), channel_id=1, source_target_pairs={{0,5},{1,4},{2,7},{3,6},{4,1},{5,0},{6,3},{7,2},{8,13},{9,12},{10,... | collective-permute-start | bytes 122888 | tf_op jit(solution)/shard_map/ppermute | solution.py:25
  20.6 2.1 %collective-permute-done.7 = f32[80,128]{1,0:T(8,128)S(1)} collective-permute-done((f32[80,128]{1,0:T(8,128)S(1)}, f32[80,128]{1,0:T(8,128)S(1)}, u32[]{:S(2)}, u32[]{:S(2)}) %collective-permute-start.7) | collective-permute-done | bytes 40992 | tf_op jit(solution)/shard_map/ppermute | solution.py:25
  22.8 1.3 %collective-permute-start.8 = (f32[96,128]{1,0:T(8,128)S(1)}, f32[96,128]{1,0:T(8,128)S(1)}, u32[]{:S(2)}, u32[]{:S(2)}) collective-permute-start(f32[96,128]{1,0:T(8,128)S(1)} %pad_maximum_fusion), channel_id=1, source_target_pairs={{0,3},{1,8},{2,11},{3,0},{4,13},{5,6},{6,5},{7,14},{8,1},{9,10},{1... | collective-permute-start | bytes 147464 | tf_op jit(solution)/shard_map/ppermute | solution.py:25
  24.1 2.2 %collective-permute-done.8 = f32[96,128]{1,0:T(8,128)S(1)} collective-permute-done((f32[96,128]{1,0:T(8,128)S(1)}, f32[96,128]{1,0:T(8,128)S(1)}, u32[]{:S(2)}, u32[]{:S(2)}) %collective-permute-start.8) | collective-permute-done | bytes 49184 | tf_op jit(solution)/shard_map/ppermute | solution.py:25
  26.4 0.0 copy-start
  26.4 0.0 copy-start.1
  26.4 0.0 copy-start.2
  26.4 0.0 copy-start.3
  26.5 0.0 copy-start.4
  26.5 0.0 copy-start.5
  26.5 1.5 %section_two.1 = (f32[64,128]{1,0:T(8,128)S(1)}, f32[8,128]{1,0:T(8,128)S(1)}) custom-call(f32[2,8,128]{2,1,0:T(8,128)S(4)} %get-tuple-element.26.tables, f32[64,128]{1,0:T(8,128)S(1)} %slice_add_fusion.lifted, f32[64,128]{1,0:T(8,128)S(1)} %get-tuple-element.36.rate_one, f32[64,128]{1,0:T(8,128)S(1)} %bitcast.119, ...), custom_call_target="tpu_custom_call" | custom-call | tf_op jit(solution)/shard_map/section_two/pallas_call | solution.py:351
  28.0 2.5 %collective-permute-start.9 = (f32[32,128]{1,0:T(8,128)S(1)}, f32[32,128]{1,0:T(8,128)S(1)}, u32[]{:S(2)}, u32[]{:S(2)}) collective-permute-start(f32[32,128]{1,0:T(8,128)S(1)} %get-tuple-element.55), channel_id=1, source_target_pairs={{0,9},{1,8},{2,11},{3,10},{4,13},{5,12},{6,15},{7,14},{8,1},{9,0},... | collective-permute-start | bytes 49160 | tf_op jit(solution)/shard_map/ppermute | solution.py:25
  30.4 1.7 %collective-permute-done.9 = f32[32,128]{1,0:T(8,128)S(1)} collective-permute-done((f32[32,128]{1,0:T(8,128)S(1)}, f32[32,128]{1,0:T(8,128)S(1)}, u32[]{:S(2)}, u32[]{:S(2)}) %collective-permute-start.9) | collective-permute-done | bytes 16416 | tf_op jit(solution)/shard_map/ppermute | solution.py:25
  32.1 1.6 %collective-permute-start.10 = (f32[16,128]{1,0:T(8,128)S(1)}, f32[16,128]{1,0:T(8,128)S(1)}, u32[]{:S(2)}, u32[]{:S(2)}) collective-permute-start(f32[16,128]{1,0:T(8,128)S(1)} %select_bitcast_fusion), channel_id=1, source_target_pairs={{0,5},{1,4},{2,7},{3,6},{4,1},{5,0},{6,3},{7,2},{8,13},{9,12},{10,... | collective-permute-start | bytes 24584 | tf_op jit(solution)/shard_map/ppermute | solution.py:25
  33.7 0.2 near_two.1
  33.8 0.3 collective-permute-start.12
  34.1 1.1 %collective-permute-done.10 = f32[16,128]{1,0:T(8,128)S(1)} collective-permute-done((f32[16,128]{1,0:T(8,128)S(1)}, f32[16,128]{1,0:T(8,128)S(1)}, u32[]{:S(2)}, u32[]{:S(2)}) %collective-permute-start.10) | collective-permute-done | bytes 8224 | tf_op jit(solution)/shard_map/ppermute | solution.py:25
  35.3 1.3 %collective-permute-start.11 = (f32[8,128]{1,0:T(8,128)S(1)}, f32[8,128]{1,0:T(8,128)S(1)}, u32[]{:S(2)}, u32[]{:S(2)}) collective-permute-start(f32[8,128]{1,0:T(8,128)S(1)} %get-tuple-element.40), channel_id=1, source_target_pairs={{0,3},{1,2},{2,1},{3,0},{4,7},{5,6},{6,5},{7,4},{8,11},{9,10},{10,... | collective-permute-start | bytes 12296 | tf_op jit(solution)/shard_map/ppermute | solution.py:25
  36.6 0.0 collective-permute-done.12
  36.6 1.8 %collective-permute-done.11 = f32[8,128]{1,0:T(8,128)S(1)} collective-permute-done((f32[8,128]{1,0:T(8,128)S(1)}, f32[8,128]{1,0:T(8,128)S(1)}, u32[]{:S(2)}, u32[]{:S(2)}) %collective-permute-start.11) | collective-permute-done | bytes 4128 | tf_op jit(solution)/shard_map/ppermute | solution.py:25
  38.4 0.0 copy-done
  38.4 0.0 copy-done.1
  38.4 0.0 copy-done.2
  38.4 0.0 copy-done.3
  38.4 0.0 copy-done.4
  38.4 0.0 copy-done.5
  38.4 0.6 %add_bitcast_fusion = (f32[1024]{0:T(1024)}, f32[1024]{0:T(1024)}) fusion(f32[8,128]{1,0:T(8,128)S(1)} %get-tuple-element.37.mid_rate, f32[1024]{0:T(1024)S(1)} %copy-done.5, f32[1024]{0:T(1024)S(1)} %copy-done.1, f32[1024]{0:T(1024)S(1)} %copy-done, f32[8,128]{1,0:T(8,128)S(1)} %near_two.1, f32[8,128]{1,0:T(8,128)S(1)} %collective-permute-done.12, ...), kind=kLoop, calls=%fused_computation.42 | loop fusion | flops 26624 | bytes 58368 | tf_op jit(solution)/shard_map/reshape | solution.py:387
  (31 shorter events, 0.2 us)
Async XLA Ops:
  0.6 12.7 %collective-permute-start.4 = (f32[88,48,128]{2,1,0:T(8,128)}, f32[88,48,128]{2,1,0:T(8,128)S(1)}, u32[]{:S(2)}, u32[]{:S(2)}) collective-permute-start(f32[88,48,128]{2,1,0:T(8,128)} %bitcast.126), channel_id=1, source_target_pairs={{0,1},{1,0},{2,3},{3,2},{4,5},{5,4},{6,7},{7,6},{8,9},{9,8},{10,11... | collective-permute-start | bytes 6488072 | tf_op jit(solution)/shard_map/ppermute | solution.py:16
  1.1 12.2 %collective-permute-start.5 = (f32[88,48,128]{2,1,0:T(8,128)}, f32[88,48,128]{2,1,0:T(8,128)S(1)}, u32[]{:S(2)}, u32[]{:S(2)}) collective-permute-start(f32[88,48,128]{2,1,0:T(8,128)} %bitcast.129), channel_id=1, source_target_pairs={{0,1},{1,0},{2,3},{3,2},{4,5},{5,4},{6,7},{7,6},{8,9},{9,8},{10,11... | collective-permute-start | bytes 6488072 | tf_op jit(solution)/shard_map/ppermute | solution.py:16
  1.2 5.7 %collective-permute-start.1 = (f32[8,128]{1,0:T(8,128)}, f32[8,128]{1,0:T(8,128)S(1)}, u32[]{:S(2)}, u32[]{:S(2)}) collective-permute-start(f32[8,128]{1,0:T(8,128)} %bitcast.135), channel_id=1, source_target_pairs={{0,9},{1,8},{2,11},{3,10},{4,13},{5,12},{6,15},{7,14},{8,1},{9,0},... | collective-permute-start | bytes 12296 | tf_op jit(solution)/shard_map/ppermute | solution.py:25
  6.5 3.4 %collective-permute-start = (f32[6,8,128]{2,1,0:T(8,128)S(1)}, f32[6,8,128]{2,1,0:T(8,128)S(1)}, u32[]{:S(2)}, u32[]{:S(2)}) collective-permute-start(f32[6,8,128]{2,1,0:T(8,128)S(1)} %pad_maximum_fusion.5.given), channel_id=1, source_target_pairs={{0,1},{1,0},{2,3},{3,2},{4,5},{5,4},{6,7},{7,6},{8,9},{9,8},{10,11... | collective-permute-start | bytes 73736 | tf_op jit(solution)/shard_map/ppermute | solution.py:16
  7.0 3.1 %collective-permute-start.2 = (f32[16,128]{1,0:T(8,128)S(1)}, f32[16,128]{1,0:T(8,128)S(1)}, u32[]{:S(2)}, u32[]{:S(2)}) collective-permute-start(f32[16,128]{1,0:T(8,128)S(1)} %maximum_bitcast_fusion.own), channel_id=1, source_target_pairs={{0,5},{1,4},{2,7},{3,6},{4,1},{5,0},{6,3},{7,2},{8,13},{9,12},{10,... | collective-permute-start | bytes 24584 | tf_op jit(solution)/shard_map/ppermute | solution.py:25
  10.1 3.2 %collective-permute-start.3 = (f32[32,128]{1,0:T(8,128)S(1)}, f32[32,128]{1,0:T(8,128)S(1)}, u32[]{:S(2)}, u32[]{:S(2)}) collective-permute-start(f32[32,128]{1,0:T(8,128)S(1)} %bitcast.121), channel_id=1, source_target_pairs={{0,3},{1,2},{2,1},{3,0},{4,7},{5,6},{6,5},{7,4},{8,11},{9,10},{10,... | collective-permute-start | bytes 49160 | tf_op jit(solution)/shard_map/ppermute | solution.py:25
  14.9 4.3 %collective-permute-start.6 = (f32[72,128]{1,0:T(8,128)S(1)}, f32[72,128]{1,0:T(8,128)S(1)}, u32[]{:S(2)}, u32[]{:S(2)}) collective-permute-start(f32[72,128]{1,0:T(8,128)S(1)} %pad_maximum_fusion.2), channel_id=1, source_target_pairs={{0,9},{1,2},{2,1},{3,10},{4,7},{5,12},{6,15},{7,4},{8,11},{9,0},{1... | collective-permute-start | bytes 110600 | tf_op jit(solution)/shard_map/ppermute | solution.py:25
  19.3 3.5 %collective-permute-start.7 = (f32[80,128]{1,0:T(8,128)S(1)}, f32[80,128]{1,0:T(8,128)S(1)}, u32[]{:S(2)}, u32[]{:S(2)}) collective-permute-start(f32[80,128]{1,0:T(8,128)S(1)} %pad_maximum_fusion.1), channel_id=1, source_target_pairs={{0,5},{1,4},{2,7},{3,6},{4,1},{5,0},{6,3},{7,2},{8,13},{9,12},{10,... | collective-permute-start | bytes 122888 | tf_op jit(solution)/shard_map/ppermute | solution.py:25
  22.8 3.6 %collective-permute-start.8 = (f32[96,128]{1,0:T(8,128)S(1)}, f32[96,128]{1,0:T(8,128)S(1)}, u32[]{:S(2)}, u32[]{:S(2)}) collective-permute-start(f32[96,128]{1,0:T(8,128)S(1)} %pad_maximum_fusion), channel_id=1, source_target_pairs={{0,3},{1,8},{2,11},{3,0},{4,13},{5,6},{6,5},{7,14},{8,1},{9,10},{1... | collective-permute-start | bytes 147464 | tf_op jit(solution)/shard_map/ppermute | solution.py:25
  26.4 12.0 %copy-start = (f32[1024]{0:T(1024)S(1)}, f32[1024]{0:T(1024)}, u32[]{:S(2)}) copy-start(f32[1024]{0:T(1024)} %param.12) | copy-start | bytes 12292
  26.4 11.9 %copy-start.1 = (f32[1024]{0:T(1024)S(1)}, f32[1024]{0:T(1024)}, u32[]{:S(2)}) copy-start(f32[1024]{0:T(1024)} %param.13) | copy-start | bytes 12292
  26.4 11.9 %copy-start.2 = (f32[1024]{0:T(1024)S(1)}, f32[1024]{0:T(1024)}, u32[]{:S(2)}) copy-start(f32[1024]{0:T(1024)} %param.14) | copy-start | bytes 12292
  26.4 11.9 %copy-start.3 = (f32[1024]{0:T(1024)S(1)}, f32[1024]{0:T(1024)}, u32[]{:S(2)}) copy-start(f32[1024]{0:T(1024)} %param.15) | copy-start | bytes 12292
  26.5 11.9 %copy-start.4 = (f32[1024]{0:T(1024)S(1)}, f32[1024]{0:T(1024)}, u32[]{:S(2)}) copy-start(f32[1024]{0:T(1024)} %param.16) | copy-start | bytes 12292
  26.5 11.9 %copy-start.5 = (f32[1024]{0:T(1024)S(1)}, f32[1024]{0:T(1024)}, u32[]{:S(2)}) copy-start(f32[1024]{0:T(1024)} %param.17) | copy-start | bytes 12292
  28.0 4.1 %collective-permute-start.9 = (f32[32,128]{1,0:T(8,128)S(1)}, f32[32,128]{1,0:T(8,128)S(1)}, u32[]{:S(2)}, u32[]{:S(2)}) collective-permute-start(f32[32,128]{1,0:T(8,128)S(1)} %get-tuple-element.55), channel_id=1, source_target_pairs={{0,9},{1,8},{2,11},{3,10},{4,13},{5,12},{6,15},{7,14},{8,1},{9,0},... | collective-permute-start | bytes 49160 | tf_op jit(solution)/shard_map/ppermute | solution.py:25
  32.1 3.1 %collective-permute-start.10 = (f32[16,128]{1,0:T(8,128)S(1)}, f32[16,128]{1,0:T(8,128)S(1)}, u32[]{:S(2)}, u32[]{:S(2)}) collective-permute-start(f32[16,128]{1,0:T(8,128)S(1)} %select_bitcast_fusion), channel_id=1, source_target_pairs={{0,5},{1,4},{2,7},{3,6},{4,1},{5,0},{6,3},{7,2},{8,13},{9,12},{10,... | collective-permute-start | bytes 24584 | tf_op jit(solution)/shard_map/ppermute | solution.py:25
  33.8 2.8 %collective-permute-start.12 = (f32[8,128]{1,0:T(8,128)S(1)}, f32[8,128]{1,0:T(8,128)S(1)}, u32[]{:S(2)}, u32[]{:S(2)}) collective-permute-start(f32[8,128]{1,0:T(8,128)S(1)} %near_two.1), channel_id=1, source_target_pairs={{0,1},{1,0},{2,3},{3,2},{4,5},{5,4},{6,7},{7,6},{8,9},{9,8},{10,11... | collective-permute-start | bytes 12296 | tf_op jit(solution)/shard_map/ppermute | solution.py:16
  35.3 3.1 %collective-permute-start.11 = (f32[8,128]{1,0:T(8,128)S(1)}, f32[8,128]{1,0:T(8,128)S(1)}, u32[]{:S(2)}, u32[]{:S(2)}) collective-permute-start(f32[8,128]{1,0:T(8,128)S(1)} %get-tuple-element.40), channel_id=1, source_target_pairs={{0,3},{1,2},{2,1},{3,0},{4,7},{5,6},{6,5},{7,4},{8,11},{9,10},{10,... | collective-permute-start | bytes 12296 | tf_op jit(solution)/shard_map/ppermute | solution.py:25

commit v4 on v3

--- a/solution.py
+++ b/solution.py
@@ -117,9 +117,32 @@
     lift[...] = (given[1] + given_other[1]) + (b_in[...] * state_rate - load_in[...] - log_values * inverse)
 
 
-def near_kernel(mid_rate, near, out, rate):
-    rate[...] = jnp.exp(mid_rate[...])
-    out[...] = near_rows(rate, near)
+def finish_kernel(
+    mid_rate, log_rate, log_state, load, a_sigma, b_sigma, log_dc, near,
+    near_two, base_two, gain_two, new_log_state, rate,
+    log_rate_in, log_state_in, load_in, a_in, b_in, dc_in, sems,
+):
+    run_copies(
+        [
+            (log_rate, log_rate_in),
+            (log_state, log_state_in),
+            (load, load_in),
+            (a_sigma, a_in),
+            (b_sigma, b_in),
+            (log_dc, dc_in),
+        ],
+        sems,
+    )
+    mid = mid_rate[...]
+    rate[...] = jnp.exp(mid)
+    near_two[...] = near_rows(rate, near)
+    states = log_state_in[...]
+    state_one = jnp.exp(-states) - jnp.exp(log_rate_in[...] - dc_in[...])
+    state_two = jnp.exp(-(states + time_step * state_one)) - jnp.exp(mid - dc_in[...])
+    gain = 0.5 * time_step / (a_in[...] + damping * rate[...])
+    gain_two[...] = gain
+    base_two[...] = 0.5 * (log_rate_in[...] + mid) + gain * (load_in[...] - b_in[...] * state_two)
+    new_log_state[...] = states + 0.5 * time_step * (state_one + state_two)
 
 
 def split_three(x):
@@ -358,23 +381,15 @@
         name="section_two",
     )(tables, part, rate_one, all_a, *known)
 
-    near_two = pl.pallas_call(
-        near_kernel,
-        out_shape=in_vmem(*per_own),
-        in_specs=[vmem, vmem],
-        out_specs=vmem,
-        scratch_shapes=[in_vmem(*per_own)],
-        compiler_params=limits,
-        name="near_two",
-    )(mid_rate, near)
+    near_two, base_two, gain_two, new_log_state = hold(
+        finish_kernel,
+        "finish",
+        [in_vmem(*per_own)] * 4,
+        [log_rate, log_state, load, a_sigma, b_sigma, log_dc],
+        [mid_rate, near],
+        [in_vmem(*per_own)] * 7 + [sems(6)],
+    )
     near_two = near_two + swap_cores(near_two)
-
-    state_one = jnp.exp(-log_state) - jnp.exp(log_rate - log_dc)
-    mid_state = log_state + time_step * state_one
-    state_two = jnp.exp(-mid_state) - jnp.exp(mid_rate - log_dc)
-    gain_two = 0.5 * time_step / (a_sigma + damping * jnp.exp(mid_rate))
-    base_two = 0.5 * (log_rate + mid_rate) + gain_two * (load - b_sigma * state_two)
-    new_log_state = log_state + 0.5 * time_step * (state_one + state_two)
 
     part = part.reshape((2,) * depth + per_own)
     for axis in range(depth):

time: 39.2 us -> 39.1 us (level)
  waiting for transfers between devices: 11.6 us -> 10.3 us
  Pallas kernels: 7.6 us -> 8.42 us
  local copies, waits for them, and re-layouts: 0.04 us -> 0.59 us
    ppermute x9, waiting for transfers between devices: 11.6 us -> 10.3 us  [swap_owners(): return lax.ppermute(x, ('blk', 'sub'), pairs)]
    pallas_call x3 -> x4, Pallas kernels: 4.53 us -> 5.51 us  [hold(): pl.pallas_call(kernel, out_shape=tuple(out_shape), in_specs=[vmem] * len(...]
    unnamed x12 -> x1, local copies, waits for them, and re-layouts: 0.04 us -> 0.59 us
  transfers between devices with their start and end apart: 13 -> 13, of which waited for: 8 -> 8; matrix products, arithmetic and copies ran while one was open for 0% -> 2% of each run, Pallas kernels for 12% -> 14%
where the time goes in v4:
time: 39.1 us; the launch traced here: 38.9 us
  starting transfers between devices  18 us (46%)
  waiting for transfers between devices  10.3 us (26%)
  Pallas kernels  8.42 us (22%)
  other arithmetic  0.8 us (2%)
  between operations  0.79 us (2%)
  local copies, waits for them, and re-layouts  0.59 us (2%)
    ppermute x9, starting transfers between devices, swap_owners(): return lax.ppermute(x, ('blk', 'sub'), pairs)  16.7 us
    ppermute x9, waiting for transfers between devices, swap_owners(): return lax.ppermute(x, ('blk', 'sub'), pairs)  10.3 us
    pallas_call x4, Pallas kernels, hold(): pl.pallas_call(kernel, out_shape=tuple(out_shape), in_specs=[vmem] * len(...  5.51 us
    pallas_call x1, Pallas kernels, shards(): pl.pallas_call(second_kernel, out_shape=(in_vmem(clusters, leaf), in_vmem...  1.46 us
    pallas_call x1, Pallas kernels, shards(): pl.pallas_call(first_kernel, out_shape=(in_vmem(clusters, leaf), in_vmem(...  1.45 us
    ppermute x4, starting transfers between devices, swap_cores(): return lax.ppermute(x, 'sub', [(0, 1), (1, 0)])  1.36 us
  transfers between devices with their start and end apart: 13, of which 8 were waited for; matrix products, arithmetic and copies ran while one was open for 2% of the time, Pallas kernels for 14%

profile of v4, /device:TPU:0, one launch (start us, length us, event | category | flops | bytes accessed | tf_op | source)
XLA Modules:
  0.0 38.9 jit_solution(697223568373191151)
XLA Ops:
  0.6 0.5 %collective-permute-start.4 = (f32[88,48,128]{2,1,0:T(8,128)}, f32[88,48,128]{2,1,0:T(8,128)S(1)}, u32[]{:S(2)}, u32[]{:S(2)}) collective-permute-start(f32[88,48,128]{2,1,0:T(8,128)} %bitcast.117), channel_id=1, source_target_pairs={{0,1},{1,0},{2,3},{3,2},{4,5},{5,4},{6,7},{7,6},{8,9},{9,8},{10,11... | collective-permute-start | bytes 6488072 | tf_op jit(solution)/shard_map/ppermute | solution.py:16
  1.1 0.1 collective-permute-start.5
  1.2 3.7 %collective-permute-start.1 = (f32[8,128]{1,0:T(8,128)}, f32[8,128]{1,0:T(8,128)S(1)}, u32[]{:S(2)}, u32[]{:S(2)}) collective-permute-start(f32[8,128]{1,0:T(8,128)} %bitcast.126), channel_id=1, source_target_pairs={{0,9},{1,8},{2,11},{3,10},{4,13},{5,12},{6,15},{7,14},{8,1},{9,0},... | collective-permute-start | bytes 12296 | tf_op jit(solution)/shard_map/ppermute | solution.py:25
  4.9 1.5 %hold_first.1 = (f32[8,128]{1,0:T(8,128)S(1)}, f32[8,128]{1,0:T(8,128)S(1)}, f32[8,128]{1,0:T(8,128)S(1)}, s32[4,8,128]{2,1,0:T(8,128)S(1)}, f32[4,128,128]{2,1,0:T(8,128)S(1)}, /*index=5*/f32[32,48,128]{2,1,0:T(8,128)S(1)}) custom-call(s32[8,1,88]{2,1,0:T(1,128)} %columns_all.1, s32[8,1,88]{2,1,0:T(1,128)} %rows_all.1, s32[1,1,88]{2,1,0:T(1,128)} %ranks.1, ...), custom_call_target="tpu_custom_call" | custom-call | bytes 4194304 | tf_op jit(solution)/shard_map/hold_first/pallas_call | solution.py:278
  6.5 0.5 %collective-permute-start = (f32[6,8,128]{2,1,0:T(8,128)S(1)}, f32[6,8,128]{2,1,0:T(8,128)S(1)}, u32[]{:S(2)}, u32[]{:S(2)}) collective-permute-start(f32[6,8,128]{2,1,0:T(8,128)S(1)} %pad_maximum_fusion.5.given), channel_id=1, source_target_pairs={{0,1},{1,0},{2,3},{3,2},{4,5},{5,4},{6,7},{7,6},{8,9},{9,8},{10,11... | collective-permute-start | bytes 73736 | tf_op jit(solution)/shard_map/ppermute | solution.py:16
  7.0 0.0 collective-permute-done.1
  7.0 1.3 %collective-permute-start.2 = (f32[16,128]{1,0:T(8,128)S(1)}, f32[16,128]{1,0:T(8,128)S(1)}, u32[]{:S(2)}, u32[]{:S(2)}) collective-permute-start(f32[16,128]{1,0:T(8,128)S(1)} %maximum_bitcast_fusion.own), channel_id=1, source_target_pairs={{0,5},{1,4},{2,7},{3,6},{4,1},{5,0},{6,3},{7,2},{8,13},{9,12},{10,... | collective-permute-start | bytes 24584 | tf_op jit(solution)/shard_map/ppermute | solution.py:25
  8.3 1.5 %hold_second.1 = (f32[56,48,128]{2,1,0:T(8,128)S(1)}, f32[24,48,128]{2,1,0:T(8,128)S(1)}, f32[16,128]{1,0:T(8,128)S(1)}) custom-call(f32[88,48,128]{2,1,0:T(8,128)} %bitcast.119, f32[88,48,128]{2,1,0:T(8,128)} %bitcast.121, f32[16,128]{1,0:T(8,128)S(1)} %maximum_bitcast_fusion.own), custom_call_target="tpu_custom_call" | custom-call | bytes 4194304 | tf_op jit(solution)/shard_map/hold_second/pallas_call | solution.py:278
  9.8 0.0 collective-permute-done.given_other
  9.8 0.3 collective-permute-done.2
  10.1 1.3 %collective-permute-start.3 = (f32[32,128]{1,0:T(8,128)S(1)}, f32[32,128]{1,0:T(8,128)S(1)}, u32[]{:S(2)}, u32[]{:S(2)}) collective-permute-start(f32[32,128]{1,0:T(8,128)S(1)} %bitcast.112), channel_id=1, source_target_pairs={{0,3},{1,2},{2,1},{3,0},{4,7},{5,6},{6,5},{7,4},{8,11},{9,10},{10,... | collective-permute-start | bytes 49160 | tf_op jit(solution)/shard_map/ppermute | solution.py:25
  11.5 1.5 %hold_third.1 = (f32[2,8,128]{2,1,0:T(8,128)S(4)}, bf16[2,64,88]{2,1,0:T(8,128)(2,1)S(1)}, f32[64,48,128]{2,1,0:T(8,128)S(1)}, f32[8,128]{1,0:T(8,128)S(1)}, f32...) custom-call(f32[6,8,128]{2,1,0:T(8,128)S(1)} %pad_maximum_fusion.5.given, f32[6,8,128]{2,1,0:T(8,128)S(1)} %collective-permute-done.given_other, ...), custom_call_target="tpu_custom_call" | custom-call | bytes 4194304 | tf_op jit(solution)/shard_map/hold_third/pallas_call | solution.py:278
  13.0 0.3 collective-permute-done.3
  13.4 0.0 collective-permute-done.4.refs_5_
  13.4 0.0 collective-permute-done.5.refs_6_
  13.4 1.5 %section_one.1 = (f32[64,128]{1,0:T(8,128)S(1)}, f32[64,128]{1,0:T(8,128)S(1)}) custom-call(f32[2,8,128]{2,1,0:T(8,128)S(4)} %get-tuple-element.30.tables, f32[64,128]{1,0:T(8,128)S(1)} %bitcast.111, f32[8,128]{1,0:T(8,128)S(1)} %get-tuple-element.32.lift, bf16[2,64,88]{2,1,0:T(8,128)(2,1)S(1)} %get-tuple-element.33.refs_0_, ...), custom_call_target="tpu_custom_call" | custom-call | tf_op jit(solution)/shard_map/section_one/pallas_call | solution.py:350
  14.9 2.3 %collective-permute-start.6 = (f32[72,128]{1,0:T(8,128)S(1)}, f32[72,128]{1,0:T(8,128)S(1)}, u32[]{:S(2)}, u32[]{:S(2)}) collective-permute-start(f32[72,128]{1,0:T(8,128)S(1)} %pad_maximum_fusion.2), channel_id=1, source_target_pairs={{0,9},{1,2},{2,1},{3,10},{4,7},{5,12},{6,15},{7,4},{8,11},{9,0},{1... | collective-permute-start | bytes 110600 | tf_op jit(solution)/shard_map/ppermute | solution.py:25
  17.1 2.1 %collective-permute-done.6 = f32[72,128]{1,0:T(8,128)S(1)} collective-permute-done((f32[72,128]{1,0:T(8,128)S(1)}, f32[72,128]{1,0:T(8,128)S(1)}, u32[]{:S(2)}, u32[]{:S(2)}) %collective-permute-start.6) | collective-permute-done | bytes 36896 | tf_op jit(solution)/shard_map/ppermute | solution.py:25
  19.3 1.4 %collective-permute-start.7 = (f32[80,128]{1,0:T(8,128)S(1)}, f32[80,128]{1,0:T(8,128)S(1)}, u32[]{:S(2)}, u32[]{:S(2)}) collective-permute-start(f32[80,128]{1,0:T(8,128)S(1)} %pad_maximum_fusion.1), channel_id=1, source_target_pairs={{0,5},{1,4},{2,7},{3,6},{4,1},{5,0},{6,3},{7,2},{8,13},{9,12},{10,... | collective-permute-start | bytes 122888 | tf_op jit(solution)/shard_map/ppermute | solution.py:25
  20.6 2.1 %collective-permute-done.7 = f32[80,128]{1,0:T(8,128)S(1)} collective-permute-done((f32[80,128]{1,0:T(8,128)S(1)}, f32[80,128]{1,0:T(8,128)S(1)}, u32[]{:S(2)}, u32[]{:S(2)}) %collective-permute-start.7) | collective-permute-done | bytes 40992 | tf_op jit(solution)/shard_map/ppermute | solution.py:25
  22.8 1.3 %collective-permute-start.8 = (f32[96,128]{1,0:T(8,128)S(1)}, f32[96,128]{1,0:T(8,128)S(1)}, u32[]{:S(2)}, u32[]{:S(2)}) collective-permute-start(f32[96,128]{1,0:T(8,128)S(1)} %pad_maximum_fusion), channel_id=1, source_target_pairs={{0,3},{1,8},{2,11},{3,0},{4,13},{5,6},{6,5},{7,14},{8,1},{9,10},{1... | collective-permute-start | bytes 147464 | tf_op jit(solution)/shard_map/ppermute | solution.py:25
  24.1 2.2 %collective-permute-done.8 = f32[96,128]{1,0:T(8,128)S(1)} collective-permute-done((f32[96,128]{1,0:T(8,128)S(1)}, f32[96,128]{1,0:T(8,128)S(1)}, u32[]{:S(2)}, u32[]{:S(2)}) %collective-permute-start.8) | collective-permute-done | bytes 49184 | tf_op jit(solution)/shard_map/ppermute | solution.py:25
  26.4 1.5 %section_two.1 = (f32[64,128]{1,0:T(8,128)S(1)}, f32[8,128]{1,0:T(8,128)S(1)}) custom-call(f32[2,8,128]{2,1,0:T(8,128)S(4)} %get-tuple-element.30.tables, f32[64,128]{1,0:T(8,128)S(1)} %slice_add_fusion.lifted, f32[64,128]{1,0:T(8,128)S(1)} %get-tuple-element.40.rate_one, f32[64,128]{1,0:T(8,128)S(1)} %bitcast.110, ...), custom_call_target="tpu_custom_call" | custom-call | tf_op jit(solution)/shard_map/section_two/pallas_call | solution.py:374
  27.9 2.5 %collective-permute-start.9 = (f32[32,128]{1,0:T(8,128)S(1)}, f32[32,128]{1,0:T(8,128)S(1)}, u32[]{:S(2)}, u32[]{:S(2)}) collective-permute-start(f32[32,128]{1,0:T(8,128)S(1)} %get-tuple-element.63), channel_id=1, source_target_pairs={{0,9},{1,8},{2,11},{3,10},{4,13},{5,12},{6,15},{7,14},{8,1},{9,0},... | collective-permute-start | bytes 49160 | tf_op jit(solution)/shard_map/ppermute | solution.py:25
  30.3 1.7 %collective-permute-done.9 = f32[32,128]{1,0:T(8,128)S(1)} collective-permute-done((f32[32,128]{1,0:T(8,128)S(1)}, f32[32,128]{1,0:T(8,128)S(1)}, u32[]{:S(2)}, u32[]{:S(2)}) %collective-permute-start.9) | collective-permute-done | bytes 16416 | tf_op jit(solution)/shard_map/ppermute | solution.py:25
  32.0 1.5 %collective-permute-start.10 = (f32[16,128]{1,0:T(8,128)S(1)}, f32[16,128]{1,0:T(8,128)S(1)}, u32[]{:S(2)}, u32[]{:S(2)}) collective-permute-start(f32[16,128]{1,0:T(8,128)S(1)} %select_bitcast_fusion), channel_id=1, source_target_pairs={{0,5},{1,4},{2,7},{3,6},{4,1},{5,0},{6,3},{7,2},{8,13},{9,12},{10,... | collective-permute-start | bytes 24584 | tf_op jit(solution)/shard_map/ppermute | solution.py:25
  33.6 1.0 %finish.1 = (f32[8,128]{1,0:T(8,128)S(1)}, f32[8,128]{1,0:T(8,128)S(1)}, f32[8,128]{1,0:T(8,128)S(1)}, f32[8,128]{1,0:T(8,128)S(1)}) custom-call(f32[8,128]{1,0:T(8,128)S(1)} %get-tuple-element.41.mid_rate, f32[8,128]{1,0:T(8,128)} %bitcast.129, f32[8,128]{1,0:T(8,128)} %bitcast.131, f32[8,128]{1,0:T(8,128)} %bitcast.133, f32[8,128]{1,0:T(8,128)} %bitcast.135, ...), custom_call_target="tpu_custom_call" | custom-call | bytes 4194304 | tf_op jit(solution)/shard_map/finish/pallas_call | solution.py:278
  34.6 0.3 collective-permute-start.12
  34.8 0.3 collective-permute-done.10
  35.2 1.3 %collective-permute-start.11 = (f32[8,128]{1,0:T(8,128)S(1)}, f32[8,128]{1,0:T(8,128)S(1)}, u32[]{:S(2)}, u32[]{:S(2)}) collective-permute-start(f32[8,128]{1,0:T(8,128)S(1)} %get-tuple-element.48), channel_id=1, source_target_pairs={{0,3},{1,2},{2,1},{3,0},{4,7},{5,6},{6,5},{7,4},{8,11},{9,10},{10,... | collective-permute-start | bytes 12296 | tf_op jit(solution)/shard_map/ppermute | solution.py:25
  36.5 0.6 %copy.24 = f32[1024]{0:T(1024)} copy(f32[1024]{0:T(1024)S(1)} %bitcast.109) | data formatting | bytes 8192
  37.1 0.0 collective-permute-done.12
  37.1 1.2 %collective-permute-done.11 = f32[8,128]{1,0:T(8,128)S(1)} collective-permute-done((f32[8,128]{1,0:T(8,128)S(1)}, f32[8,128]{1,0:T(8,128)S(1)}, u32[]{:S(2)}, u32[]{:S(2)}) %collective-permute-start.11) | collective-permute-done | bytes 4128 | tf_op jit(solution)/shard_map/ppermute | solution.py:25
  38.3 0.6 %fusion.8 = f32[1024]{0:T(1024)} fusion(f32[8,128]{1,0:T(8,128)S(1)} %get-tuple-element.43, f32[8,128]{1,0:T(8,128)S(1)} %get-tuple-element.44, f32[8,128]{1,0:T(8,128)S(1)} %collective-permute-done.11, f32[8,128]{1,0:T(8,128)S(1)} %get-tuple-element.46, f32[8,128]{1,0:T(8,128)S(1)} %collective-permute-done.12, pred[1,8,128]{2,1,0:T(8,128)(4,1)S(1)} %get-tuple-element.49, ...), kind=kLoop, calls=%fused_computation.34 | loop fusion | flops 6144 | bytes 33792 | tf_op jit(solution)/shard_map/reshape | solution.py:402
  (31 shorter events, 0.2 us)
Async XLA Ops:
  0.6 12.7 %collective-permute-start.4 = (f32[88,48,128]{2,1,0:T(8,128)}, f32[88,48,128]{2,1,0:T(8,128)S(1)}, u32[]{:S(2)}, u32[]{:S(2)}) collective-permute-start(f32[88,48,128]{2,1,0:T(8,128)} %bitcast.117), channel_id=1, source_target_pairs={{0,1},{1,0},{2,3},{3,2},{4,5},{5,4},{6,7},{7,6},{8,9},{9,8},{10,11... | collective-permute-start | bytes 6488072 | tf_op jit(solution)/shard_map/ppermute | solution.py:16
  1.1 12.2 %collective-permute-start.5 = (f32[88,48,128]{2,1,0:T(8,128)}, f32[88,48,128]{2,1,0:T(8,128)S(1)}, u32[]{:S(2)}, u32[]{:S(2)}) collective-permute-start(f32[88,48,128]{2,1,0:T(8,128)} %bitcast.120), channel_id=1, source_target_pairs={{0,1},{1,0},{2,3},{3,2},{4,5},{5,4},{6,7},{7,6},{8,9},{9,8},{10,11... | collective-permute-start | bytes 6488072 | tf_op jit(solution)/shard_map/ppermute | solution.py:16
  1.2 5.7 %collective-permute-start.1 = (f32[8,128]{1,0:T(8,128)}, f32[8,128]{1,0:T(8,128)S(1)}, u32[]{:S(2)}, u32[]{:S(2)}) collective-permute-start(f32[8,128]{1,0:T(8,128)} %bitcast.126), channel_id=1, source_target_pairs={{0,9},{1,8},{2,11},{3,10},{4,13},{5,12},{6,15},{7,14},{8,1},{9,0},... | collective-permute-start | bytes 12296 | tf_op jit(solution)/shard_map/ppermute | solution.py:25
  6.5 3.4 %collective-permute-start = (f32[6,8,128]{2,1,0:T(8,128)S(1)}, f32[6,8,128]{2,1,0:T(8,128)S(1)}, u32[]{:S(2)}, u32[]{:S(2)}) collective-permute-start(f32[6,8,128]{2,1,0:T(8,128)S(1)} %pad_maximum_fusion.5.given), channel_id=1, source_target_pairs={{0,1},{1,0},{2,3},{3,2},{4,5},{5,4},{6,7},{7,6},{8,9},{9,8},{10,11... | collective-permute-start | bytes 73736 | tf_op jit(solution)/shard_map/ppermute | solution.py:16
  7.0 3.1 %collective-permute-start.2 = (f32[16,128]{1,0:T(8,128)S(1)}, f32[16,128]{1,0:T(8,128)S(1)}, u32[]{:S(2)}, u32[]{:S(2)}) collective-permute-start(f32[16,128]{1,0:T(8,128)S(1)} %maximum_bitcast_fusion.own), channel_id=1, source_target_pairs={{0,5},{1,4},{2,7},{3,6},{4,1},{5,0},{6,3},{7,2},{8,13},{9,12},{10,... | collective-permute-start | bytes 24584 | tf_op jit(solution)/shard_map/ppermute | solution.py:25
  10.1 3.2 %collective-permute-start.3 = (f32[32,128]{1,0:T(8,128)S(1)}, f32[32,128]{1,0:T(8,128)S(1)}, u32[]{:S(2)}, u32[]{:S(2)}) collective-permute-start(f32[32,128]{1,0:T(8,128)S(1)} %bitcast.112), channel_id=1, source_target_pairs={{0,3},{1,2},{2,1},{3,0},{4,7},{5,6},{6,5},{7,4},{8,11},{9,10},{10,... | collective-permute-start | bytes 49160 | tf_op jit(solution)/shard_map/ppermute | solution.py:25
  14.9 4.3 %collective-permute-start.6 = (f32[72,128]{1,0:T(8,128)S(1)}, f32[72,128]{1,0:T(8,128)S(1)}, u32[]{:S(2)}, u32[]{:S(2)}) collective-permute-start(f32[72,128]{1,0:T(8,128)S(1)} %pad_maximum_fusion.2), channel_id=1, source_target_pairs={{0,9},{1,2},{2,1},{3,10},{4,7},{5,12},{6,15},{7,4},{8,11},{9,0},{1... | collective-permute-start | bytes 110600 | tf_op jit(solution)/shard_map/ppermute | solution.py:25
  19.3 3.5 %collective-permute-start.7 = (f32[80,128]{1,0:T(8,128)S(1)}, f32[80,128]{1,0:T(8,128)S(1)}, u32[]{:S(2)}, u32[]{:S(2)}) collective-permute-start(f32[80,128]{1,0:T(8,128)S(1)} %pad_maximum_fusion.1), channel_id=1, source_target_pairs={{0,5},{1,4},{2,7},{3,6},{4,1},{5,0},{6,3},{7,2},{8,13},{9,12},{10,... | collective-permute-start | bytes 122888 | tf_op jit(solution)/shard_map/ppermute | solution.py:25
  22.8 3.6 %collective-permute-start.8 = (f32[96,128]{1,0:T(8,128)S(1)}, f32[96,128]{1,0:T(8,128)S(1)}, u32[]{:S(2)}, u32[]{:S(2)}) collective-permute-start(f32[96,128]{1,0:T(8,128)S(1)} %pad_maximum_fusion), channel_id=1, source_target_pairs={{0,3},{1,8},{2,11},{3,0},{4,13},{5,6},{6,5},{7,14},{8,1},{9,10},{1... | collective-permute-start | bytes 147464 | tf_op jit(solution)/shard_map/ppermute | solution.py:25
  27.9 4.1 %collective-permute-start.9 = (f32[32,128]{1,0:T(8,128)S(1)}, f32[32,128]{1,0:T(8,128)S(1)}, u32[]{:S(2)}, u32[]{:S(2)}) collective-permute-start(f32[32,128]{1,0:T(8,128)S(1)} %get-tuple-element.63), channel_id=1, source_target_pairs={{0,9},{1,8},{2,11},{3,10},{4,13},{5,12},{6,15},{7,14},{8,1},{9,0},... | collective-permute-start | bytes 49160 | tf_op jit(solution)/shard_map/ppermute | solution.py:25
  32.0 3.1 %collective-permute-start.10 = (f32[16,128]{1,0:T(8,128)S(1)}, f32[16,128]{1,0:T(8,128)S(1)}, u32[]{:S(2)}, u32[]{:S(2)}) collective-permute-start(f32[16,128]{1,0:T(8,128)S(1)} %select_bitcast_fusion), channel_id=1, source_target_pairs={{0,5},{1,4},{2,7},{3,6},{4,1},{5,0},{6,3},{7,2},{8,13},{9,12},{10,... | collective-permute-start | bytes 24584 | tf_op jit(solution)/shard_map/ppermute | solution.py:25
  34.6 2.5 %collective-permute-start.12 = (f32[8,128]{1,0:T(8,128)S(1)}, f32[8,128]{1,0:T(8,128)S(1)}, u32[]{:S(2)}, u32[]{:S(2)}) collective-permute-start(f32[8,128]{1,0:T(8,128)S(1)} %get-tuple-element.46), channel_id=1, source_target_pairs={{0,1},{1,0},{2,3},{3,2},{4,5},{5,4},{6,7},{7,6},{8,9},{9,8},{10,11... | collective-permute-start | bytes 12296 | tf_op jit(solution)/shard_map/ppermute | solution.py:16
  35.2 3.1 %collective-permute-start.11 = (f32[8,128]{1,0:T(8,128)S(1)}, f32[8,128]{1,0:T(8,128)S(1)}, u32[]{:S(2)}, u32[]{:S(2)}) collective-permute-start(f32[8,128]{1,0:T(8,128)S(1)} %get-tuple-element.48), channel_id=1, source_target_pairs={{0,3},{1,2},{2,1},{3,0},{4,7},{5,6},{6,5},{7,4},{8,11},{9,10},{10,... | collective-permute-start | bytes 12296 | tf_op jit(solution)/shard_map/ppermute | solution.py:25

commit v5 on v4

--- a/solution.py
+++ b/solution.py
@@ -241,11 +241,11 @@
     def by_kind(even, odd):
         return jnp.where(flags[depth] != 0, odd, even)
 
-    def set_at(step):
-        return by_kind(flags[depth - 1 - even_axes[step]], flags[depth - 1 - odd_axes[step]]) != 0
-
-    def hop(x, step):
-        return swap_owners(x, bit_of(even_axes[step]), bit_of(odd_axes[step]))
+    def set_at(axes):
+        return by_kind(*(flags[depth - 1 - axis] for axis in axes)) != 0
+
+    def hop(x, axes):
+        return swap_owners(x, *(bit_of(axis) for axis in axes))
 
     def rest(axes):
         return list(axes) + [depth, depth + 1]
@@ -287,7 +287,7 @@
         )(*vmem_args[:-1], *(in_hbm(x) for x in hbm_args), *vmem_args[-1:])
 
     columns_a = blocks // 11 * 4
-    rows_a = blocks // 11 * 3
+    rows_a = blocks // 11 * 4
 
     def factor_part(count):
         return in_vmem(count, kmax, leaf)
@@ -358,10 +358,10 @@
     )(tables, rates, lift, *known)
 
     all_a = own_a[None]
-    for step in range(depth):
-        other = hop(jnp.concatenate([part, flat(all_a)], axis=0), step)
+    for axes in zip(even_axes, odd_axes):
+        other = hop(jnp.concatenate([part, flat(all_a)], axis=0), axes)
         part = part + other[:clusters]
-        all_a = joined(set_at(step), 0, all_a, other[clusters:].reshape(all_a.shape))
+        all_a = joined(set_at(axes), 0, all_a, other[clusters:].reshape(all_a.shape))
     all_a = all_a.reshape((2,) * depth + per_own)
     all_a = by_kind(
         *(
@@ -391,13 +391,13 @@
     )
     near_two = near_two + swap_cores(near_two)
 
+    last_even, last_odd = even_axes, even_axes[:1] + even_axes[:0:-1]
     part = part.reshape((2,) * depth + per_own)
-    for axis in range(depth):
-        low = lax.slice_in_dim(part, 0, 1, axis=axis)
-        high = lax.slice_in_dim(part, 1, 2, axis=axis)
-        send = jnp.where(set_in(axis), low, high)
-        keep = jnp.where(set_in(axis), high, low)
-        part = keep + swap_owners(flat(send), bit_of(axis)).reshape(keep.shape)
+    part = by_kind(jnp.transpose(part, rest(last_even)), jnp.transpose(part, rest(last_odd)))
+    for axes in zip(last_even, last_odd):
+        flag = set_at(axes)
+        send, keep = jnp.where(flag, part[0], part[1]), jnp.where(flag, part[1], part[0])
+        part = keep + hop(flat(send), axes).reshape(keep.shape)
     new_log_rate = base_two - gain_two * (part.reshape(per_own) + near_two)
     return (new_log_rate.reshape(-1), new_log_state.reshape(-1))
 

time: 39.1 us -> 39.1 us (level)
  no operation moved by 1% of the time
where the time goes in v5:
time: 39.1 us; the launch traced here: 38.9 us
  starting transfers between devices  18.1 us (46%)
  waiting for transfers between devices  10.1 us (26%)
  Pallas kernels  8.38 us (21%)
  between operations  0.83 us (2%)
  other arithmetic  0.81 us (2%)
  local copies, waits for them, and re-layouts  0.6 us (2%)
    ppermute x9, starting transfers between devices, swap_owners(): return lax.ppermute(x, ('blk', 'sub'), pairs)  16.7 us
    ppermute x9, waiting for transfers between devices, swap_owners(): return lax.ppermute(x, ('blk', 'sub'), pairs)  10.1 us
    pallas_call x4, Pallas kernels, hold(): pl.pallas_call(kernel, out_shape=tuple(out_shape), in_specs=[vmem] * len(...  5.51 us
    ppermute x4, starting transfers between devices, swap_cores(): return lax.ppermute(x, 'sub', [(0, 1), (1, 0)])  1.47 us
    pallas_call x1, Pallas kernels, shards(): pl.pallas_call(second_kernel, out_shape=(in_vmem(clusters, leaf), in_vmem...  1.44 us
    pallas_call x1, Pallas kernels, shards(): pl.pallas_call(first_kernel, out_shape=(in_vmem(clusters, leaf), in_vmem(...  1.43 us
  transfers between devices with their start and end apart: 13, of which 8 were waited for; matrix products, arithmetic and copies ran while one was open for 2% of the time, Pallas kernels for 14%

profile of v5, /device:TPU:0, one launch (start us, length us, event | category | flops | bytes accessed | tf_op | source)
XLA Modules:
  0.0 38.9 jit_solution(4528385456654273249)
XLA Ops:
  0.6 0.5 %collective-permute-start.4 = (f32[88,48,128]{2,1,0:T(8,128)}, f32[88,48,128]{2,1,0:T(8,128)S(1)}, u32[]{:S(2)}, u32[]{:S(2)}) collective-permute-start(f32[88,48,128]{2,1,0:T(8,128)} %bitcast.145), channel_id=1, source_target_pairs={{0,1},{1,0},{2,3},{3,2},{4,5},{5,4},{6,7},{7,6},{8,9},{9,8},{10,11... | collective-permute-start | bytes 6488072 | tf_op jit(solution)/shard_map/ppermute | solution.py:16
  1.1 0.1 collective-permute-start.5
  1.2 3.7 %collective-permute-start.1 = (f32[8,128]{1,0:T(8,128)}, f32[8,128]{1,0:T(8,128)S(1)}, u32[]{:S(2)}, u32[]{:S(2)}) collective-permute-start(f32[8,128]{1,0:T(8,128)} %bitcast.152), channel_id=1, source_target_pairs={{0,9},{1,8},{2,11},{3,10},{4,13},{5,12},{6,15},{7,14},{8,1},{9,0},... | collective-permute-start | bytes 12296 | tf_op jit(solution)/shard_map/ppermute | solution.py:25
  4.9 1.5 %hold_first.1 = (f32[8,128]{1,0:T(8,128)S(1)}, f32[8,128]{1,0:T(8,128)S(1)}, f32[8,128]{1,0:T(8,128)S(1)}, s32[4,8,128]{2,1,0:T(8,128)S(1)}, f32[4,128,128]{2,1,0:T(8,128)S(1)}, /*index=5*/f32[32,48,128]{2,1,0:T(8,128)S(1)}) custom-call(s32[8,1,88]{2,1,0:T(1,128)} %columns_all.1, s32[8,1,88]{2,1,0:T(1,128)} %rows_all.1, s32[1,1,88]{2,1,0:T(1,128)} %ranks.1, ...), custom_call_target="tpu_custom_call" | custom-call | bytes 4194304 | tf_op jit(solution)/shard_map/hold_first/pallas_call | solution.py:278
  6.5 0.5 %collective-permute-start = (f32[6,8,128]{2,1,0:T(8,128)S(1)}, f32[6,8,128]{2,1,0:T(8,128)S(1)}, u32[]{:S(2)}, u32[]{:S(2)}) collective-permute-start(f32[6,8,128]{2,1,0:T(8,128)S(1)} %pad_maximum_fusion.5.given), channel_id=1, source_target_pairs={{0,1},{1,0},{2,3},{3,2},{4,5},{5,4},{6,7},{7,6},{8,9},{9,8},{10,11... | collective-permute-start | bytes 73736 | tf_op jit(solution)/shard_map/ppermute | solution.py:16
  7.0 0.0 collective-permute-done.1
  7.0 1.3 %collective-permute-start.2 = (f32[16,128]{1,0:T(8,128)S(1)}, f32[16,128]{1,0:T(8,128)S(1)}, u32[]{:S(2)}, u32[]{:S(2)}) collective-permute-start(f32[16,128]{1,0:T(8,128)S(1)} %maximum_bitcast_fusion.own), channel_id=1, source_target_pairs={{0,5},{1,4},{2,7},{3,6},{4,1},{5,0},{6,3},{7,2},{8,13},{9,12},{10,... | collective-permute-start | bytes 24584 | tf_op jit(solution)/shard_map/ppermute | solution.py:25
  8.3 1.6 %hold_second.1 = (f32[56,48,128]{2,1,0:T(8,128)S(1)}, f32[32,48,128]{2,1,0:T(8,128)S(1)}, f32[16,128]{1,0:T(8,128)S(1)}) custom-call(f32[88,48,128]{2,1,0:T(8,128)} %bitcast.147, f32[88,48,128]{2,1,0:T(8,128)} %bitcast.149, f32[16,128]{1,0:T(8,128)S(1)} %maximum_bitcast_fusion.own), custom_call_target="tpu_custom_call" | custom-call | bytes 4194304 | tf_op jit(solution)/shard_map/hold_second/pallas_call | solution.py:278
  9.9 0.0 collective-permute-done.given_other
  9.9 0.2 collective-permute-done.2
  10.2 1.4 %collective-permute-start.3 = (f32[32,128]{1,0:T(8,128)S(1)}, f32[32,128]{1,0:T(8,128)S(1)}, u32[]{:S(2)}, u32[]{:S(2)}) collective-permute-start(f32[32,128]{1,0:T(8,128)S(1)} %bitcast.140), channel_id=1, source_target_pairs={{0,3},{1,2},{2,1},{3,0},{4,7},{5,6},{6,5},{7,4},{8,11},{9,10},{10,... | collective-permute-start | bytes 49160 | tf_op jit(solution)/shard_map/ppermute | solution.py:25
  11.6 1.5 %hold_third.1 = (f32[2,8,128]{2,1,0:T(8,128)S(4)}, bf16[2,64,88]{2,1,0:T(8,128)(2,1)S(1)}, f32[56,48,128]{2,1,0:T(8,128)S(1)}, f32[8,128]{1,0:T(8,128)S(1)}, f32...) custom-call(f32[6,8,128]{2,1,0:T(8,128)S(1)} %pad_maximum_fusion.5.given, f32[6,8,128]{2,1,0:T(8,128)S(1)} %collective-permute-done.given_other, ...), custom_call_target="tpu_custom_call" | custom-call | bytes 4194304 | tf_op jit(solution)/shard_map/hold_third/pallas_call | solution.py:278
  13.0 0.3 collective-permute-done.3
  13.4 0.0 collective-permute-done.4.refs_5_
  13.4 0.0 collective-permute-done.5.refs_6_
  13.4 1.4 %section_one.1 = (f32[64,128]{1,0:T(8,128)S(1)}, f32[64,128]{1,0:T(8,128)S(1)}) custom-call(f32[2,8,128]{2,1,0:T(8,128)S(4)} %get-tuple-element.30.tables, f32[64,128]{1,0:T(8,128)S(1)} %bitcast.137, f32[8,128]{1,0:T(8,128)S(1)} %get-tuple-element.32.lift, bf16[2,64,88]{2,1,0:T(8,128)(2,1)S(1)} %get-tuple-element.33.refs_0_, ...), custom_call_target="tpu_custom_call" | custom-call | tf_op jit(solution)/shard_map/section_one/pallas_call | solution.py:350
  14.9 2.3 %collective-permute-start.6 = (f32[72,128]{1,0:T(8,128)S(1)}, f32[72,128]{1,0:T(8,128)S(1)}, u32[]{:S(2)}, u32[]{:S(2)}) collective-permute-start(f32[72,128]{1,0:T(8,128)S(1)} %pad_maximum_fusion.2), channel_id=1, source_target_pairs={{0,9},{1,2},{2,1},{3,10},{4,7},{5,12},{6,15},{7,4},{8,11},{9,0},{1... | collective-permute-start | bytes 110600 | tf_op jit(solution)/shard_map/ppermute | solution.py:25
  17.2 2.0 %collective-permute-done.6 = f32[72,128]{1,0:T(8,128)S(1)} collective-permute-done((f32[72,128]{1,0:T(8,128)S(1)}, f32[72,128]{1,0:T(8,128)S(1)}, u32[]{:S(2)}, u32[]{:S(2)}) %collective-permute-start.6) | collective-permute-done | bytes 36896 | tf_op jit(solution)/shard_map/ppermute | solution.py:25
  19.3 1.4 %collective-permute-start.7 = (f32[80,128]{1,0:T(8,128)S(1)}, f32[80,128]{1,0:T(8,128)S(1)}, u32[]{:S(2)}, u32[]{:S(2)}) collective-permute-start(f32[80,128]{1,0:T(8,128)S(1)} %pad_maximum_fusion.1), channel_id=1, source_target_pairs={{0,5},{1,4},{2,7},{3,6},{4,1},{5,0},{6,3},{7,2},{8,13},{9,12},{10,... | collective-permute-start | bytes 122888 | tf_op jit(solution)/shard_map/ppermute | solution.py:25
  20.6 2.1 %collective-permute-done.7 = f32[80,128]{1,0:T(8,128)S(1)} collective-permute-done((f32[80,128]{1,0:T(8,128)S(1)}, f32[80,128]{1,0:T(8,128)S(1)}, u32[]{:S(2)}, u32[]{:S(2)}) %collective-permute-start.7) | collective-permute-done | bytes 40992 | tf_op jit(solution)/shard_map/ppermute | solution.py:25
  22.8 1.4 %collective-permute-start.8 = (f32[96,128]{1,0:T(8,128)S(1)}, f32[96,128]{1,0:T(8,128)S(1)}, u32[]{:S(2)}, u32[]{:S(2)}) collective-permute-start(f32[96,128]{1,0:T(8,128)S(1)} %pad_maximum_fusion), channel_id=1, source_target_pairs={{0,3},{1,8},{2,11},{3,0},{4,13},{5,6},{6,5},{7,14},{8,1},{9,10},{1... | collective-permute-start | bytes 147464 | tf_op jit(solution)/shard_map/ppermute | solution.py:25
  24.2 2.2 %collective-permute-done.8 = f32[96,128]{1,0:T(8,128)S(1)} collective-permute-done((f32[96,128]{1,0:T(8,128)S(1)}, f32[96,128]{1,0:T(8,128)S(1)}, u32[]{:S(2)}, u32[]{:S(2)}) %collective-permute-start.8) | collective-permute-done | bytes 49184 | tf_op jit(solution)/shard_map/ppermute | solution.py:25
  26.4 1.4 %section_two.1 = (f32[64,128]{1,0:T(8,128)S(1)}, f32[8,128]{1,0:T(8,128)S(1)}) custom-call(f32[2,8,128]{2,1,0:T(8,128)S(4)} %get-tuple-element.30.tables, f32[64,128]{1,0:T(8,128)S(1)} %slice_add_fusion.lifted, f32[64,128]{1,0:T(8,128)S(1)} %get-tuple-element.40.rate_one, f32[64,128]{1,0:T(8,128)S(1)} %bitcast.136, ...), custom_call_target="tpu_custom_call" | custom-call | tf_op jit(solution)/shard_map/section_two/pallas_call | solution.py:374
  27.9 2.4 %collective-permute-start.9 = (f32[32,128]{1,0:T(8,128)S(1)}, f32[32,128]{1,0:T(8,128)S(1)}, u32[]{:S(2)}, u32[]{:S(2)}) collective-permute-start(f32[32,128]{1,0:T(8,128)S(1)} %bitcast_select_fusion.1), channel_id=1, source_target_pairs={{0,9},{1,8},{2,11},{3,10},{4,13},{5,12},{6,15},{7,14},{8,1},{9,0},... | collective-permute-start | bytes 49160 | tf_op jit(solution)/shard_map/ppermute | solution.py:25
  30.3 1.7 %collective-permute-done.9 = f32[32,128]{1,0:T(8,128)S(1)} collective-permute-done((f32[32,128]{1,0:T(8,128)S(1)}, f32[32,128]{1,0:T(8,128)S(1)}, u32[]{:S(2)}, u32[]{:S(2)}) %collective-permute-start.9) | collective-permute-done | bytes 16416 | tf_op jit(solution)/shard_map/ppermute | solution.py:25
  32.0 1.4 %collective-permute-start.10 = (f32[16,128]{1,0:T(8,128)S(1)}, f32[16,128]{1,0:T(8,128)S(1)}, u32[]{:S(2)}, u32[]{:S(2)}) collective-permute-start(f32[16,128]{1,0:T(8,128)S(1)} %bitcast_select_fusion.3), channel_id=1, source_target_pairs={{0,5},{1,2},{2,1},{3,6},{4,7},{5,0},{6,3},{7,4},{8,11},{9,12},{10,... | collective-permute-start | bytes 24584 | tf_op jit(solution)/shard_map/ppermute | solution.py:25
  33.4 1.0 %finish.1 = (f32[8,128]{1,0:T(8,128)S(1)}, f32[8,128]{1,0:T(8,128)S(1)}, f32[8,128]{1,0:T(8,128)S(1)}, f32[8,128]{1,0:T(8,128)S(1)}) custom-call(f32[8,128]{1,0:T(8,128)S(1)} %get-tuple-element.41.mid_rate, f32[8,128]{1,0:T(8,128)} %bitcast.155, f32[8,128]{1,0:T(8,128)} %bitcast.157, f32[8,128]{1,0:T(8,128)} %bitcast.159, f32[8,128]{1,0:T(8,128)} %bitcast.161, ...), custom_call_target="tpu_custom_call" | custom-call | bytes 4194304 | tf_op jit(solution)/shard_map/finish/pallas_call | solution.py:278
  34.4 0.4 collective-permute-start.12
  34.8 0.4 %collective-permute-done.10 = f32[16,128]{1,0:T(8,128)S(1)} collective-permute-done((f32[16,128]{1,0:T(8,128)S(1)}, f32[16,128]{1,0:T(8,128)S(1)}, u32[]{:S(2)}, u32[]{:S(2)}) %collective-permute-start.10) | collective-permute-done | bytes 8224 | tf_op jit(solution)/shard_map/ppermute | solution.py:25
  35.2 1.4 %collective-permute-start.11 = (f32[8,128]{1,0:T(8,128)S(1)}, f32[8,128]{1,0:T(8,128)S(1)}, u32[]{:S(2)}, u32[]{:S(2)}) collective-permute-start(f32[8,128]{1,0:T(8,128)S(1)} %get-tuple-element.48), channel_id=1, source_target_pairs={{0,3},{1,4},{2,7},{3,0},{4,1},{5,6},{6,5},{7,2},{8,13},{9,10},{10,... | collective-permute-start | bytes 12296 | tf_op jit(solution)/shard_map/ppermute | solution.py:25
  36.6 0.6 %copy.36 = f32[1024]{0:T(1024)} copy(f32[1024]{0:T(1024)S(1)} %bitcast.135) | data formatting | bytes 8192
  37.2 0.0 collective-permute-done.12
  37.2 1.1 %collective-permute-done.11 = f32[8,128]{1,0:T(8,128)S(1)} collective-permute-done((f32[8,128]{1,0:T(8,128)S(1)}, f32[8,128]{1,0:T(8,128)S(1)}, u32[]{:S(2)}, u32[]{:S(2)}) %collective-permute-start.11) | collective-permute-done | bytes 4128 | tf_op jit(solution)/shard_map/ppermute | solution.py:25
  38.3 0.6 %subtract_bitcast_fusion = f32[1024]{0:T(1024)} fusion(f32[8,128]{1,0:T(8,128)S(1)} %get-tuple-element.43, f32[8,128]{1,0:T(8,128)S(1)} %get-tuple-element.44, f32[8,128]{1,0:T(8,128)S(1)} %get-tuple-element.46, f32[8,128]{1,0:T(8,128)S(1)} %collective-permute-done.12, f32[8,128]{1,0:T(8,128)S(1)} %collective-permute-done.11, ...), kind=kLoop, calls=%fused_computation.47 | loop fusion | flops 6144 | bytes 33792 | tf_op jit(solution)/shard_map/reshape | solution.py:402
  (33 shorter events, 0.2 us)
Async XLA Ops:
  0.6 12.8 %collective-permute-start.4 = (f32[88,48,128]{2,1,0:T(8,128)}, f32[88,48,128]{2,1,0:T(8,128)S(1)}, u32[]{:S(2)}, u32[]{:S(2)}) collective-permute-start(f32[88,48,128]{2,1,0:T(8,128)} %bitcast.145), channel_id=1, source_target_pairs={{0,1},{1,0},{2,3},{3,2},{4,5},{5,4},{6,7},{7,6},{8,9},{9,8},{10,11... | collective-permute-start | bytes 6488072 | tf_op jit(solution)/shard_map/ppermute | solution.py:16
  1.1 12.3 %collective-permute-start.5 = (f32[88,48,128]{2,1,0:T(8,128)}, f32[88,48,128]{2,1,0:T(8,128)S(1)}, u32[]{:S(2)}, u32[]{:S(2)}) collective-permute-start(f32[88,48,128]{2,1,0:T(8,128)} %bitcast.148), channel_id=1, source_target_pairs={{0,1},{1,0},{2,3},{3,2},{4,5},{5,4},{6,7},{7,6},{8,9},{9,8},{10,11... | collective-permute-start | bytes 6488072 | tf_op jit(solution)/shard_map/ppermute | solution.py:16
  1.2 5.7 %collective-permute-start.1 = (f32[8,128]{1,0:T(8,128)}, f32[8,128]{1,0:T(8,128)S(1)}, u32[]{:S(2)}, u32[]{:S(2)}) collective-permute-start(f32[8,128]{1,0:T(8,128)} %bitcast.152), channel_id=1, source_target_pairs={{0,9},{1,8},{2,11},{3,10},{4,13},{5,12},{6,15},{7,14},{8,1},{9,0},... | collective-permute-start | bytes 12296 | tf_op jit(solution)/shard_map/ppermute | solution.py:25
  6.5 3.4 %collective-permute-start = (f32[6,8,128]{2,1,0:T(8,128)S(1)}, f32[6,8,128]{2,1,0:T(8,128)S(1)}, u32[]{:S(2)}, u32[]{:S(2)}) collective-permute-start(f32[6,8,128]{2,1,0:T(8,128)S(1)} %pad_maximum_fusion.5.given), channel_id=1, source_target_pairs={{0,1},{1,0},{2,3},{3,2},{4,5},{5,4},{6,7},{7,6},{8,9},{9,8},{10,11... | collective-permute-start | bytes 73736 | tf_op jit(solution)/shard_map/ppermute | solution.py:16
  7.0 3.1 %collective-permute-start.2 = (f32[16,128]{1,0:T(8,128)S(1)}, f32[16,128]{1,0:T(8,128)S(1)}, u32[]{:S(2)}, u32[]{:S(2)}) collective-permute-start(f32[16,128]{1,0:T(8,128)S(1)} %maximum_bitcast_fusion.own), channel_id=1, source_target_pairs={{0,5},{1,4},{2,7},{3,6},{4,1},{5,0},{6,3},{7,2},{8,13},{9,12},{10,... | collective-permute-start | bytes 24584 | tf_op jit(solution)/shard_map/ppermute | solution.py:25
  10.2 3.2 %collective-permute-start.3 = (f32[32,128]{1,0:T(8,128)S(1)}, f32[32,128]{1,0:T(8,128)S(1)}, u32[]{:S(2)}, u32[]{:S(2)}) collective-permute-start(f32[32,128]{1,0:T(8,128)S(1)} %bitcast.140), channel_id=1, source_target_pairs={{0,3},{1,2},{2,1},{3,0},{4,7},{5,6},{6,5},{7,4},{8,11},{9,10},{10,... | collective-permute-start | bytes 49160 | tf_op jit(solution)/shard_map/ppermute | solution.py:25
  14.9 4.3 %collective-permute-start.6 = (f32[72,128]{1,0:T(8,128)S(1)}, f32[72,128]{1,0:T(8,128)S(1)}, u32[]{:S(2)}, u32[]{:S(2)}) collective-permute-start(f32[72,128]{1,0:T(8,128)S(1)} %pad_maximum_fusion.2), channel_id=1, source_target_pairs={{0,9},{1,2},{2,1},{3,10},{4,7},{5,12},{6,15},{7,4},{8,11},{9,0},{1... | collective-permute-start | bytes 110600 | tf_op jit(solution)/shard_map/ppermute | solution.py:25
  19.3 3.5 %collective-permute-start.7 = (f32[80,128]{1,0:T(8,128)S(1)}, f32[80,128]{1,0:T(8,128)S(1)}, u32[]{:S(2)}, u32[]{:S(2)}) collective-permute-start(f32[80,128]{1,0:T(8,128)S(1)} %pad_maximum_fusion.1), channel_id=1, source_target_pairs={{0,5},{1,4},{2,7},{3,6},{4,1},{5,0},{6,3},{7,2},{8,13},{9,12},{10,... | collective-permute-start | bytes 122888 | tf_op jit(solution)/shard_map/ppermute | solution.py:25
  22.8 3.6 %collective-permute-start.8 = (f32[96,128]{1,0:T(8,128)S(1)}, f32[96,128]{1,0:T(8,128)S(1)}, u32[]{:S(2)}, u32[]{:S(2)}) collective-permute-start(f32[96,128]{1,0:T(8,128)S(1)} %pad_maximum_fusion), channel_id=1, source_target_pairs={{0,3},{1,8},{2,11},{3,0},{4,13},{5,6},{6,5},{7,14},{8,1},{9,10},{1... | collective-permute-start | bytes 147464 | tf_op jit(solution)/shard_map/ppermute | solution.py:25
  27.9 4.1 %collective-permute-start.9 = (f32[32,128]{1,0:T(8,128)S(1)}, f32[32,128]{1,0:T(8,128)S(1)}, u32[]{:S(2)}, u32[]{:S(2)}) collective-permute-start(f32[32,128]{1,0:T(8,128)S(1)} %bitcast_select_fusion.1), channel_id=1, source_target_pairs={{0,9},{1,8},{2,11},{3,10},{4,13},{5,12},{6,15},{7,14},{8,1},{9,0},... | collective-permute-start | bytes 49160 | tf_op jit(solution)/shard_map/ppermute | solution.py:25
  32.0 3.1 %collective-permute-start.10 = (f32[16,128]{1,0:T(8,128)S(1)}, f32[16,128]{1,0:T(8,128)S(1)}, u32[]{:S(2)}, u32[]{:S(2)}) collective-permute-start(f32[16,128]{1,0:T(8,128)S(1)} %bitcast_select_fusion.3), channel_id=1, source_target_pairs={{0,5},{1,2},{2,1},{3,6},{4,7},{5,0},{6,3},{7,4},{8,11},{9,12},{10,... | collective-permute-start | bytes 24584 | tf_op jit(solution)/shard_map/ppermute | solution.py:25
  34.4 2.8 %collective-permute-start.12 = (f32[8,128]{1,0:T(8,128)S(1)}, f32[8,128]{1,0:T(8,128)S(1)}, u32[]{:S(2)}, u32[]{:S(2)}) collective-permute-start(f32[8,128]{1,0:T(8,128)S(1)} %get-tuple-element.46), channel_id=1, source_target_pairs={{0,1},{1,0},{2,3},{3,2},{4,5},{5,4},{6,7},{7,6},{8,9},{9,8},{10,11... | collective-permute-start | bytes 12296 | tf_op jit(solution)/shard_map/ppermute | solution.py:16
  35.2 3.1 %collective-permute-start.11 = (f32[8,128]{1,0:T(8,128)S(1)}, f32[8,128]{1,0:T(8,128)S(1)}, u32[]{:S(2)}, u32[]{:S(2)}) collective-permute-start(f32[8,128]{1,0:T(8,128)S(1)} %get-tuple-element.48), channel_id=1, source_target_pairs={{0,3},{1,4},{2,7},{3,0},{4,1},{5,6},{6,5},{7,2},{8,13},{9,10},{10,... | collective-permute-start | bytes 12296 | tf_op jit(solution)/shard_map/ppermute | solution.py:25
